TPU v7x, 512 devices: a whole 4x4x16 slice. The times are simulated.
512 devices in a mesh: wide: 64 (over z, y), narrow: 8 (over x, core).
Axes of the slice: x: 4, y: 4, z: 16, core: 2. Of those that a mesh axis runs over, the one named last changes fastest.
Arguments:
- column_state: float32 [16, 4, 720896], P(None, None, ('wide', 'narrow')), may hold values from -6 to 6
- diffusivity: float32 [15, 720896], P(None, ('wide', 'narrow')), may hold values from 0.05 to 5
- row_len: int32 [128], replicated, may hold values from 2576 to 5136, as said below
- lat_rows: int32 [128], P('wide'), may hold values from 0 to 127, as said below
- wave_order: int32 [1280], replicated, may hold values from 0 to 1279, each once
- tile_map: int32 [512, 1408], P(('wide', 'narrow')), may hold values from 0 to 1407, each once within a row
Outputs:
- spectra: float32 [2, 64, 128, 1280], P(None, None, 'wide', 'narrow')
Inputs may be any that keep to these rules, and one draw needn't show every extreme that they name: `row_len`: each length is 5136 minus a multiple of 4. `lat_rows`: a permutation of the row numbers. `wave_order`: a permutation of the wavenumbers. `tile_map`: each row is a permutation of the column slots.
All inputs are finite; a program needn't handle non-finite values.
Results may differ from a plain program's by a relative error of at most 0.0037.
Values may be sent and summed in bfloat16 or wider, within the bound.
No kernel may reach another device: no remote copies, remote signals or barrier semaphores. Data moves between devices by JAX's collectives and lax.ppermute only.
A program may use at most 64 MiB of HBM per device.

v0:
```python
import math

import jax
import jax.numpy as jnp
from jax import lax
from jax.sharding import PartitionSpec as P

LPAD = 5632
MW = 1280


def vertical_solve(column_state, diffusivity):
    zero_row = jnp.zeros_like(diffusivity[:1])
    below_coef = jnp.concatenate([zero_row, diffusivity], axis=0)
    above_coef = jnp.concatenate([diffusivity, zero_row], axis=0)

    def forward(carry_pair, level_items):
        ratio_prev, value_prev = carry_pair
        below, above, source = level_items
        pivot_value = 1.0 + below + above + below * ratio_prev
        ratio_now = -above / pivot_value
        value_now = (source + below * value_prev) / pivot_value
        return ((ratio_now, value_now), (ratio_now, value_now))

    start_pair = (jnp.zeros_like(diffusivity[0]), jnp.zeros_like(column_state[0]))
    unused, (ratios, values) = lax.scan(forward, start_pair, (below_coef, above_coef, column_state))

    def backward(next_value, level_items):
        ratio_now, value_now = level_items
        solved_level = value_now - ratio_now * next_value
        return (solved_level, solved_level)

    unused, solved = lax.scan(
        backward, jnp.zeros_like(column_state[0]), (ratios, values), reverse=True
    )
    return solved


def row_transform(row_values, length, wave_ids):
    slab_width = 512
    block_count = (length + slab_width - 1) // slab_width
    mode_count = wave_ids.shape[0]
    scale_angle = 2.0 * math.pi / length.astype(jnp.float32)
    positions = jnp.arange(slab_width, dtype=jnp.int32)
    residue = positions[:, None] * wave_ids[None, :] % length
    phase_angle = residue.astype(jnp.float32) * scale_angle
    base_table = jnp.concatenate([jnp.cos(phase_angle), -jnp.sin(phase_angle)], axis=1).astype(
        jnp.bfloat16
    )

    def add_block(block_index, sums_pair):
        real_sum, imag_sum = sums_pair
        first_slot = (block_index * slab_width).astype(jnp.int32)
        slab_values = lax.dynamic_slice_in_dim(row_values, first_slot, slab_width, 1)
        inside = first_slot + positions < length
        slab_values = jnp.where(inside[None, :], slab_values, jnp.zeros_like(slab_values))
        product = jnp.dot(slab_values, base_table, preferred_element_type=jnp.float32)
        cos_part = product[:, :mode_count]
        sin_part = product[:, mode_count:]
        shift_angle = (first_slot * wave_ids % length).astype(jnp.float32) * scale_angle
        twiddle_cos = jnp.cos(shift_angle)[None, :]
        twiddle_sin = jnp.sin(shift_angle)[None, :]
        real_sum = real_sum + twiddle_cos * cos_part + twiddle_sin * sin_part
        imag_sum = imag_sum + twiddle_cos * sin_part - twiddle_sin * cos_part
        return (real_sum, imag_sum)

    empty = jnp.zeros((row_values.shape[0], mode_count), jnp.float32)
    real_sum, imag_sum = lax.fori_loop(0, block_count, add_block, (empty, empty))
    return jnp.concatenate([real_sum, imag_sum], axis=1) * lax.rsqrt(length.astype(jnp.float32))


def body(column_state, diffusivity, row_len, lat_rows, wave_order, tile_map):
    solved = vertical_solve(column_state, diffusivity)
    col_count = solved.shape[2]
    field_levels = solved.shape[0] * solved.shape[1]
    wide_count = lax.axis_size("wide")
    piece_width = col_count // wide_count
    grid_cols = solved.astype(jnp.bfloat16).reshape(field_levels, col_count)
    grid_cols = jnp.take(grid_cols, tile_map[0], axis=1)
    grid_cols = grid_cols.reshape(field_levels, wide_count, piece_width)
    row_slots = lax.all_to_all(
        lax.all_to_all(grid_cols, "wide", split_axis=1, concat_axis=1, tiled=True),
        "narrow",
        split_axis=0,
        concat_axis=2,
        tiled=True,
    )
    local_levels = row_slots.shape[0]
    local_rows = lat_rows.shape[0]
    row_slots = row_slots.reshape(local_levels, local_rows, LPAD)
    row_numbers = jnp.arange(row_len.shape[0], dtype=jnp.int32)
    lengths = jnp.sum(
        jnp.where(lat_rows[:, None] == row_numbers[None, :], row_len[None, :], 0), axis=1
    )
    row_results = []
    for row_index in range(local_rows):
        row_results.append(
            row_transform(row_slots[:, row_index, :], lengths[row_index], wave_order)
        )
    spectra = jnp.stack(row_results, axis=1)
    spectra = spectra.reshape(local_levels, local_rows, 2, MW)
    spectra = jnp.transpose(spectra, (2, 0, 1, 3))
    return lax.all_to_all(spectra, "narrow", split_axis=3, concat_axis=1, tiled=True)


def solution(mesh):
    return jax.shard_map(
        body,
        mesh=mesh,
        in_specs=(
            P(None, None, ("wide", "narrow")),
            P(None, ("wide", "narrow")),
            P(),
            P("wide"),
            P(),
            P(("wide", "narrow"), None),
        ),
        out_specs=P(None, None, "wide", "narrow"),
        check_vma=False,
    )
```

profile of v0, /device:TPU:1, one launch (start us, length us, event | category | flops | bytes accessed | tf_op | source)
XLA Modules:
  0.0 213.7 jit_solution(7925641337275317636)
XLA Ops:
  0.1 0.7 fusion.44
  0.8 0.7 reduce.3
  1.5 1.0 fusion.49
  2.5 16.3 %while.66 = (s32[]{:T(128)}, f32[1408]{0:T(1024)S(1)}, f32[4,1408]{1,0:T(4,128)S(1)}, f32[16,1408]{1,0:T(8,128)S(1)}, f32[16,4,1408]{2,1,0:T(4,128)S(1)}, /*inde...) while((s32[]{:T(128)}, f32[1408]{0:T(1024)S(1)}, ...), condition=%wide.region_2.3_spmd.clone, body=%wide.region_1.2_spmd.clone.sunk | while | flops 32387 | bytes 179836 | solution.py:26
  2.6 0.8 bitcast_dynamic-update-slice_fusion.4
  3.6 0.8 bitcast_dynamic-update-slice_fusion.4
  4.7 0.8 bitcast_dynamic-update-slice_fusion.4
  5.7 0.8 bitcast_dynamic-update-slice_fusion.4
  6.7 0.8 bitcast_dynamic-update-slice_fusion.4
  7.7 0.8 bitcast_dynamic-update-slice_fusion.4
  8.7 0.8 bitcast_dynamic-update-slice_fusion.4
  9.8 0.8 bitcast_dynamic-update-slice_fusion.4
  10.8 0.8 bitcast_dynamic-update-slice_fusion.4
  11.8 0.8 bitcast_dynamic-update-slice_fusion.4
  12.8 0.8 bitcast_dynamic-update-slice_fusion.4
  13.8 0.8 bitcast_dynamic-update-slice_fusion.4
  14.9 0.8 bitcast_dynamic-update-slice_fusion.4
  15.9 0.8 bitcast_dynamic-update-slice_fusion.4
  16.9 0.8 bitcast_dynamic-update-slice_fusion.4
  17.9 0.8 bitcast_dynamic-update-slice_fusion.4
  18.9 1.4 while.67
  20.6 3.3 %gather_fusion = bf16[1408,64]{1,0:T(8,128)(2,1)S(1)} fusion(bf16[64,1408]{0,1:T(8,128)(2,1)S(1)} %copy.32, s32[2048]{0:T(1024)S(1)} %pad_clamp_fusion), kind=kCustom, calls=%fused_computation | custom fusion | bytes 366080 | tf_op jit(solution)/shard_map/jit(_take)/gather | solution.py:79
  24.5 1.0 reshape.182
  25.5 19.3 %all-to-all-start = ((bf16[64,2,704]{2,1,0:T(2,128)(2,1)}), bf16[64,2,704]{2,1,0:T(2,128)(2,1)S(1)}, u32[]{:S(2)}, u32[]{:S(2)}) async-start(bf16[64,2,704]{2,1,0:T(2,128)(2,1)} %reshape.182), calls=%async_computation | async-start | bytes 393216 | tf_op jit(solution)/shard_map/all_to_all | solution.py:82
  49.6 71.6 %cosine_convert_fusion.1 = (bf16[512,1280]{1,0:T(8,128)(2,1)}, bf16[512,1280]{1,0:T(8,128)(2,1)}, bf16[512,1280]{1,0:T(8,128)(2,1)}, bf16[512,1280]{1,0:T(8,128)(2,1)}) fusion(f32[]{:T(128)} %div.35, s32[]{:T(128)} %select_n.108, s32[1280]{0:T(1024)S(1)} %copy-done, pred[]{:T(512)} %lt.126, f32[]{:T(128)} %div.39, pred[]{:T(512)} %lt.132, s32[]{:T(128)} %select_n.114), kind=kLoop, calls=%fused_computation.61 | loop fusion | flops 16384000 | bytes 5248018 | tf_op jit(solution)/shard_map/convert.2
  122.0 0.9 reshape.184
  123.0 5.3 %all-to-all-start.1 = ((bf16[8,2,5632]{2,1,0:T(2,128)(2,1)}), bf16[8,2,5632]{2,1,0:T(2,128)(2,1)S(1)}, u32[]{:S(2)}, u32[]{:S(2)}) async-start(bf16[8,2,5632]{2,1,0:T(2,128)(2,1)} %reshape.184), calls=%async_computation.1 | async-start | bytes 360448 | tf_op jit(solution)/shard_map/all_to_all | solution.py:81
  128.2 3.7 %pad_maximum_fusion = (bf16[512,2560]{1,0:T(8,128)(2,1)}, bf16[512,2560]{1,0:T(8,128)(2,1)S(1)}) fusion(bf16[512,1280]{1,0:T(8,128)(2,1)} %get-tuple-element.606, bf16[512,1280]{1,0:T(8,128)(2,1)} %get-tuple-element.603, bf16[512,1280]{1,0:T(8,128)(2,1)} %get-tuple-element.604, bf16[512,1280]{1,0:T(8,128)(2,1)} %get-tuple-element.605), kind=kLoop, calls=%fused_computation.56 | loop fusion | flops 10485760 | bytes 10485760 | tf_op jit(solution)/shard_map/concatenate | solution.py:47
  134.3 1.6 copy.35
  135.9 3.1 %reshape.168 = bf16[8,2,5632]{2,1,0:T(2,128)(2,1)S(1)} reshape(bf16[8,64,8,22]{3,2,1,0:T(8,128)(2,1)} %copy.35) | data formatting | bytes 360448 | tf_op jit(solution)/shard_map/reshape | solution.py:90
  139.3 34.5 %while.64 = (s32[]{:T(128)}, f32[8,1280]{1,0:T(8,128)S(1)}, f32[8,1280]{1,0:T(8,128)S(1)}, s32[]{:T(128)}, s32[1280]{0:T(1024)S(1)}, /*index=5*/s32[]{:T(128)}, ...) while((s32[]{:T(128)}, f32[8,1280]{1,0:T(8,128)S(1)}, ...), condition=%wide.region_6.7_spmd.clone, body=%wide.region_5.6_spmd.clone.sunk | while | flops 21071364 | bytes 2984148 | solution.py:68
  139.4 0.7 fusion.66
  140.1 2.2 %fusion.67 = f32[8,2560]{1,0:T(8,128)S(1)} fusion(bf16[512,2560]{1,0:T(8,128)(2,1)} %get-tuple-element.1000, bf16[8,5632]{1,0:T(8,128)(2,1)S(1)} %get-tuple-element.999, s32[]{:T(128)S(6)} %select_n.182, pred[512]{0:T(512)(128)(4,1)S(1)} %fusion.66), kind=kOutput, calls=%fused_computation.8.clone.1 | convolution fusion | flops 20975616 | bytes 2712068 | tf_op jit(solution)/shard_map/while/body/dot_general | solution.py:57
  142.5 0.7 fusion.66
  143.2 2.2 %fusion.67 = f32[8,2560]{1,0:T(8,128)S(1)} fusion(bf16[512,2560]{1,0:T(8,128)(2,1)} %get-tuple-element.1000, bf16[8,5632]{1,0:T(8,128)(2,1)S(1)} %get-tuple-element.999, s32[]{:T(128)S(6)} %select_n.182, pred[512]{0:T(512)(128)(4,1)S(1)} %fusion.66), kind=kOutput, calls=%fused_computation.8.clone.1 | convolution fusion | flops 20975616 | bytes 2712068 | tf_op jit(solution)/shard_map/while/body/dot_general | solution.py:57
  145.6 0.7 fusion.66
  146.3 2.2 %fusion.67 = f32[8,2560]{1,0:T(8,128)S(1)} fusion(bf16[512,2560]{1,0:T(8,128)(2,1)} %get-tuple-element.1000, bf16[8,5632]{1,0:T(8,128)(2,1)S(1)} %get-tuple-element.999, s32[]{:T(128)S(6)} %select_n.182, pred[512]{0:T(512)(128)(4,1)S(1)} %fusion.66), kind=kOutput, calls=%fused_computation.8.clone.1 | convolution fusion | flops 20975616 | bytes 2712068 | tf_op jit(solution)/shard_map/while/body/dot_general | solution.py:57
  148.8 0.7 fusion.66
  149.5 2.2 %fusion.67 = f32[8,2560]{1,0:T(8,128)S(1)} fusion(bf16[512,2560]{1,0:T(8,128)(2,1)} %get-tuple-element.1000, bf16[8,5632]{1,0:T(8,128)(2,1)S(1)} %get-tuple-element.999, s32[]{:T(128)S(6)} %select_n.182, pred[512]{0:T(512)(128)(4,1)S(1)} %fusion.66), kind=kOutput, calls=%fused_computation.8.clone.1 | convolution fusion | flops 20975616 | bytes 2712068 | tf_op jit(solution)/shard_map/while/body/dot_general | solution.py:57
  151.9 0.7 fusion.66
  152.6 2.2 %fusion.67 = f32[8,2560]{1,0:T(8,128)S(1)} fusion(bf16[512,2560]{1,0:T(8,128)(2,1)} %get-tuple-element.1000, bf16[8,5632]{1,0:T(8,128)(2,1)S(1)} %get-tuple-element.999, s32[]{:T(128)S(6)} %select_n.182, pred[512]{0:T(512)(128)(4,1)S(1)} %fusion.66), kind=kOutput, calls=%fused_computation.8.clone.1 | convolution fusion | flops 20975616 | bytes 2712068 | tf_op jit(solution)/shard_map/while/body/dot_general | solution.py:57
  155.0 0.7 fusion.66
  155.7 2.2 %fusion.67 = f32[8,2560]{1,0:T(8,128)S(1)} fusion(bf16[512,2560]{1,0:T(8,128)(2,1)} %get-tuple-element.1000, bf16[8,5632]{1,0:T(8,128)(2,1)S(1)} %get-tuple-element.999, s32[]{:T(128)S(6)} %select_n.182, pred[512]{0:T(512)(128)(4,1)S(1)} %fusion.66), kind=kOutput, calls=%fused_computation.8.clone.1 | convolution fusion | flops 20975616 | bytes 2712068 | tf_op jit(solution)/shard_map/while/body/dot_general | solution.py:57
  158.2 0.7 fusion.66
  158.9 2.2 %fusion.67 = f32[8,2560]{1,0:T(8,128)S(1)} fusion(bf16[512,2560]{1,0:T(8,128)(2,1)} %get-tuple-element.1000, bf16[8,5632]{1,0:T(8,128)(2,1)S(1)} %get-tuple-element.999, s32[]{:T(128)S(6)} %select_n.182, pred[512]{0:T(512)(128)(4,1)S(1)} %fusion.66), kind=kOutput, calls=%fused_computation.8.clone.1 | convolution fusion | flops 20975616 | bytes 2712068 | tf_op jit(solution)/shard_map/while/body/dot_general | solution.py:57
  161.3 0.7 fusion.66
  162.0 2.2 %fusion.67 = f32[8,2560]{1,0:T(8,128)S(1)} fusion(bf16[512,2560]{1,0:T(8,128)(2,1)} %get-tuple-element.1000, bf16[8,5632]{1,0:T(8,128)(2,1)S(1)} %get-tuple-element.999, s32[]{:T(128)S(6)} %select_n.182, pred[512]{0:T(512)(128)(4,1)S(1)} %fusion.66), kind=kOutput, calls=%fused_computation.8.clone.1 | convolution fusion | flops 20975616 | bytes 2712068 | tf_op jit(solution)/shard_map/while/body/dot_general | solution.py:57
  164.5 0.7 fusion.66
  165.2 2.2 %fusion.67 = f32[8,2560]{1,0:T(8,128)S(1)} fusion(bf16[512,2560]{1,0:T(8,128)(2,1)} %get-tuple-element.1000, bf16[8,5632]{1,0:T(8,128)(2,1)S(1)} %get-tuple-element.999, s32[]{:T(128)S(6)} %select_n.182, pred[512]{0:T(512)(128)(4,1)S(1)} %fusion.66), kind=kOutput, calls=%fused_computation.8.clone.1 | convolution fusion | flops 20975616 | bytes 2712068 | tf_op jit(solution)/shard_map/while/body/dot_general | solution.py:57
  167.6 0.7 fusion.66
  168.3 2.2 %fusion.67 = f32[8,2560]{1,0:T(8,128)S(1)} fusion(bf16[512,2560]{1,0:T(8,128)(2,1)} %get-tuple-element.1000, bf16[8,5632]{1,0:T(8,128)(2,1)S(1)} %get-tuple-element.999, s32[]{:T(128)S(6)} %select_n.182, pred[512]{0:T(512)(128)(4,1)S(1)} %fusion.66), kind=kOutput, calls=%fused_computation.8.clone.1 | convolution fusion | flops 20975616 | bytes 2712068 | tf_op jit(solution)/shard_map/while/body/dot_general | solution.py:57
  170.7 0.7 fusion.66
  171.4 2.2 %fusion.67 = f32[8,2560]{1,0:T(8,128)S(1)} fusion(bf16[512,2560]{1,0:T(8,128)(2,1)} %get-tuple-element.1000, bf16[8,5632]{1,0:T(8,128)(2,1)S(1)} %get-tuple-element.999, s32[]{:T(128)S(6)} %select_n.182, pred[512]{0:T(512)(128)(4,1)S(1)} %fusion.66), kind=kOutput, calls=%fused_computation.8.clone.1 | convolution fusion | flops 20975616 | bytes 2712068 | tf_op jit(solution)/shard_map/while/body/dot_general | solution.py:57
  173.9 13.6 %while.65 = (s32[]{:T(128)}, f32[8,1280]{1,0:T(8,128)S(1)}, f32[8,1280]{1,0:T(8,128)S(1)}, s32[]{:T(128)}, s32[1280]{0:T(1024)S(1)}, /*index=5*/s32[]{:T(128)}, ...) while((s32[]{:T(128)}, f32[8,1280]{1,0:T(8,128)S(1)}, ...), condition=%wide.region_8.9_spmd.clone, body=%wide.region_7.8_spmd.clone.sunk | while | flops 21071364 | bytes 2984148 | solution.py:68
  176.8 0.6 fusion.71
  179.4 0.6 fusion.71
  183.5 0.6 fusion.71
  187.5 1.7 copy.36
  189.2 2.0 bitcast_bitcast_fusion
  191.2 5.0 %reshape.186 = f32[8,1,5120]{2,1,0:T(1,128)S(1)} reshape(f32[1280,2,2,8]{3,2,1,0:T(2,128)} %bitcast_bitcast_fusion) | data formatting | bytes 327680
  196.2 9.6 %all_to_all.38 = f32[8,1,5120]{2,1,0:T(1,128)S(1)} all-to-all(f32[8,1,5120]{2,1,0:T(1,128)S(1)} %reshape.186), channel_id=1, replica_groups=mesh['wide'=64,'narrow'=8] {'narrow'}, dimensions={0} | all-to-all | bytes 327680 | tf_op jit(solution)/shard_map/all_to_all | solution.py:103
  206.4 1.0 reduce.9
  207.4 4.0 %reshape.187 = f32[1280,2,2,8]{3,2,1,0:T(2,128)S(1)} reshape(f32[8,5120]{1,0:T(8,128)S(1)} %reduce.9) | data formatting | bytes 327680
  211.4 2.3 %copy.37 = f32[2,8,8,2,160]{4,3,2,1,0:T(2,128)} copy(f32[2,8,8,2,160]{2,0,3,4,1:T(2,128)S(1)} %bitcast.56) | data formatting | bytes 327680 | tf_op jit(solution)/shard_map/all_to_all | solution.py:103
  (191 shorter events, 21.7 us)
Async XLA Ops:
  20.3 24.5 %copy-start.1 = (s32[128]{0:T(128)S(1)}, s32[128]{0:T(128)}, u32[]{:S(2)}) copy-start(s32[128]{0:T(128)} %param.16) | copy-start | bytes 1540
  20.3 24.5 %copy-start.2 = (s32[2]{0:T(128)S(1)}, s32[2]{0:T(128)}, u32[]{:S(2)}) copy-start(s32[2]{0:T(128)} %param.17) | copy-start | bytes 28
  20.3 29.4 %copy-start = (s32[1280]{0:T(1024)S(1)}, s32[1280]{0:T(1024)}, u32[]{:S(2)}) copy-start(s32[1280]{0:T(1024)} %param.18) | copy-start | bytes 15364
  25.5 95.8 %all-to-all-start = ((bf16[64,2,704]{2,1,0:T(2,128)(2,1)}), bf16[64,2,704]{2,1,0:T(2,128)(2,1)S(1)}, u32[]{:S(2)}, u32[]{:S(2)}) async-start(bf16[64,2,704]{2,1,0:T(2,128)(2,1)} %reshape.182), calls=%async_computation | async-start | bytes 393216 | tf_op jit(solution)/shard_map/all_to_all | solution.py:82
  123.0 11.0 %all-to-all-start.1 = ((bf16[8,2,5632]{2,1,0:T(2,128)(2,1)}), bf16[8,2,5632]{2,1,0:T(2,128)(2,1)S(1)}, u32[]{:S(2)}, u32[]{:S(2)}) async-start(bf16[8,2,5632]{2,1,0:T(2,128)(2,1)} %reshape.184), calls=%async_computation.1 | async-start | bytes 360448 | tf_op jit(solution)/shard_map/all_to_all | solution.py:81
where the time goes:
time: 216 us; the launch traced here: 214 us
  other arithmetic  110 us (51%)
  local copies, waits for them, and re-layouts  32.5 us (15%)
  matrix products  28.5 us (13%)
  starting transfers between devices  24.5 us (11%)
  blocking collectives  9.63 us (4%)
  between operations  5.82 us (3%)
  loops' own time  2.39 us (1%)
    another operation x1, other arithmetic  71.6 us
    dot_general x21, matrix products, add_block(): jnp.dot(slab_values, base_table, preferred_element_type=jnp.float32)  28.5 us
    all_to_all x1, starting transfers between devices, body(): lax.all_to_all(grid_cols, 'wide', split_axis=1, concat_axis=1, tiled=True)  19.3 us
    lt x21, other arithmetic, add_block(): inside = first_slot + positions < length  14 us
    unnamed x14, local copies, waits for them, and re-layouts  13.7 us
    dynamic_update_slice x32, other arithmetic, vertical_solve(): lax.scan(forward, start_pair, (below_coef, above_coef, column_state))  12.7 us
    all_to_all x1, blocking collectives, body(): lax.all_to_all(spectra, 'narrow', split_axis=3, concat_axis=1, tiled=True)  9.63 us
    all_to_all x1, starting transfers between devices, body(): lax.all_to_all(lax.all_to_all(grid_cols, 'wide', split_axis=1, concat_axi...  5.25 us
  transfers between devices with their start and end apart: 2, of which 1 were waited for; matrix products, arithmetic and copies ran while one was open for 36% of the time, Pallas kernels for 0%

commit v1 on v0

v1 whole, which is shorter than its diff:
```python
import math

import jax
import jax.numpy as jnp
from jax import lax
from jax.experimental import pallas as pl
from jax.experimental.pallas import tpu as pltpu
from jax.sharding import Mesh, PartitionSpec as P

LEV = 16
NF = 4
FL = 64
SETS = 64
PIECE = 22
TILE_COLS = 1408
CHUNK = 12
ROWS = SETS * CHUNK
HALF = ROWS // 2
OWN = 160
LANES = 384
VMEM = 40 * 1024 * 1024


def solve_kernel(state_ref, diff_ref, map_ref, out_ref, ratio_ref, value_ref, cols_ref, slots_ref, rows_ref):
    ratio = jnp.zeros((1, TILE_COLS), jnp.float32)
    value = jnp.zeros((NF, TILE_COLS), jnp.float32)
    below = jnp.zeros((1, TILE_COLS), jnp.float32)
    for lev in range(LEV):
        if lev < LEV - 1:
            above = diff_ref[lev : lev + 1, :]
        else:
            above = jnp.zeros((1, TILE_COLS), jnp.float32)
        inverse = 1.0 / (1.0 + below + above + below * ratio)
        ratio = -above * inverse
        value = (state_ref[lev] + below * value) * inverse
        ratio_ref[lev : lev + 1, :] = ratio
        value_ref[lev] = value
        below = above
    solved = value
    cols_ref[(LEV - 1) * NF : LEV * NF, :] = solved
    for lev in range(LEV - 2, -1, -1):
        solved = value_ref[lev] - ratio_ref[lev : lev + 1, :] * solved
        cols_ref[lev * NF : (lev + 1) * NF, :] = solved
    cols = cols_ref[...].astype(jnp.bfloat16)
    cols = jnp.concatenate([cols, cols], axis=0)
    step = 256
    for first in range(0, TILE_COLS, step):
        width = min(step, TILE_COLS - first)
        ids = lax.broadcasted_iota(jnp.int32, (TILE_COLS, width), 0)
        pick = jnp.where(ids == map_ref[0:1, first : first + width], 1.0, 0.0).astype(jnp.bfloat16)
        moved = jnp.dot(cols, pick, preferred_element_type=jnp.float32)
        slots_ref[first : first + width, :] = moved.T
    low_lane = lax.broadcasted_iota(jnp.int32, (PIECE // 2, 2 * FL), 1) < FL
    zero_row = jnp.zeros((1, 2 * FL), jnp.float32)
    for s in range(SETS):
        even = slots_ref[pl.ds(s * PIECE, PIECE // 2, stride=2), :]
        odd = slots_ref[pl.ds(s * PIECE + 1, PIECE // 2, stride=2), :]
        rows_ref[s * CHUNK : s * CHUNK + PIECE // 2, :] = jnp.where(low_lane, even, odd)
        rows_ref[s * CHUNK + PIECE // 2 : (s + 1) * CHUNK, :] = zero_row
    out_ref[...] = rows_ref[...].astype(jnp.bfloat16)


def cos_sin_turns(turns):
    square = turns * turns
    s = jnp.full_like(turns, -(math.pi**11) / math.factorial(11))
    for k, sign in ((9, 1.0), (7, -1.0), (5, 1.0), (3, -1.0), (1, 1.0)):
        s = s * square + sign * math.pi**k / math.factorial(k)
    s = s * turns
    c = jnp.full_like(turns, (math.pi**12) / math.factorial(12))
    for k, sign in ((10, -1.0), (8, 1.0), (6, -1.0), (4, 1.0), (2, -1.0), (0, 1.0)):
        c = c * square + sign * math.pi**k / math.factorial(k)
    return 1.0 - 2.0 * s * s, 2.0 * s * c


def turns_of(product, length, inverse):
    return (product - jnp.floor(product * inverse + 0.5) * length) * inverse


def row_lengths(len_ref, lat_ref, r):
    return len_ref[lat_ref[r]]


def table_kernel(len_ref, lat_ref, pos_ref, wave_ref, table_ref, twiddle_ref):
    pos = pos_ref[0]
    core = lax.rem(pos, 2)
    other = pos + 1 - 2 * core
    own = wave_ref[pl.ds(pos, 1), :]
    theirs = wave_ref[pl.ds(other, 1), :]
    waves = jnp.concatenate([own, theirs, jnp.zeros((1, LANES - 2 * OWN), jnp.int32)], axis=1)
    waves = waves.astype(jnp.float32)
    block = 16
    for r in range(2):
        length = jnp.full((1, LANES), row_lengths(len_ref, lat_ref, r), jnp.int32).astype(jnp.float32)
        inverse = 1.0 / length
        scale = lax.rsqrt(length)
        scale = scale * (1.5 - 0.5 * length * scale * scale)
        for first in range(0, HALF, block):
            row = (lax.broadcasted_iota(jnp.int32, (block, LANES), 0) + first).astype(jnp.float32)
            group = jnp.floor((row + 0.5) * (1.0 / CHUNK))
            slot = 8.0 * PIECE * group + 2.0 * (row - CHUNK * group)
            cosine, sine = cos_sin_turns(turns_of(slot * waves, length, inverse))
            table_ref[r, first : first + block, 0:LANES] = cosine.astype(jnp.bfloat16)
            table_ref[r, first : first + block, LANES:] = (-sine).astype(jnp.bfloat16)
        item = lax.broadcasted_iota(jnp.int32, (8, LANES), 0)
        shift = 2 * PIECE * (item // 2) + item % 2 + PIECE * core
        cosine, sine = cos_sin_turns(turns_of(shift.astype(jnp.float32) * waves, length, inverse))
        twiddle_ref[2 * r] = cosine * scale
        twiddle_ref[2 * r + 1] = sine * scale


def transform_kernel(len_ref, lat_ref, pos_ref, rows_ref, table_ref, twiddle_ref, own_ref, theirs_ref):
    core = lax.rem(pos_ref[0], 2)
    row = lax.broadcasted_iota(jnp.int32, (HALF, 2 * FL), 0)
    lane = lax.broadcasted_iota(jnp.int32, (HALF, 2 * FL), 1)
    group = row // CHUNK
    inner = row - CHUNK * group
    slot = 8 * PIECE * group + 2 * inner + jnp.where(lane >= FL, 1, 0)
    slot = jnp.where(inner == CHUNK - 1, 1 << 20, slot)
    for r in range(2):
        length = row_lengths(len_ref, lat_ref, r)
        real = jnp.zeros((FL, LANES), jnp.float32)
        imag = jnp.zeros((FL, LANES), jnp.float32)
        for x in range(4):
            inside = slot < length - 2 * PIECE * x - PIECE * core
            values = rows_ref[x, r * HALF : (r + 1) * HALF, :].astype(jnp.float32)
            values = jnp.where(inside, values, 0.0).T.astype(jnp.bfloat16)
            product = jnp.dot(values, table_ref[r], preferred_element_type=jnp.float32)
            for p in range(2):
                cos_part = product[p * FL : (p + 1) * FL, 0:LANES]
                sin_part = product[p * FL : (p + 1) * FL, LANES:]
                tc = twiddle_ref[2 * r, 2 * x + p : 2 * x + p + 1, :]
                ts = twiddle_ref[2 * r + 1, 2 * x + p : 2 * x + p + 1, :]
                real = real + tc * cos_part + ts * sin_part
                imag = imag + tc * sin_part - ts * cos_part
        own_ref[0, r] = real[:, 0:OWN]
        own_ref[1, r] = imag[:, 0:OWN]
        theirs_ref[0, r] = real[:, OWN : 2 * OWN]
        theirs_ref[1, r] = imag[:, OWN : 2 * OWN]


def add_kernel(own_ref, got_ref, out_ref):
    for part in range(2):
        for r in range(2):
            out_ref[part, :, r, :] = own_ref[part, r] + got_ref[part, r]


def body(column_state, diffusivity, row_len, lat_rows, wave_order, tile_map):
    f32, bf16 = jnp.float32, jnp.bfloat16
    pos = (2 * lax.axis_index("x") + lax.axis_index("core")).astype(jnp.int32).reshape(1)
    smem = pl.BlockSpec(memory_space=pltpu.SMEM)
    vmem = pl.BlockSpec(memory_space=pltpu.VMEM)
    params = pltpu.CompilerParams(vmem_limit_bytes=VMEM)
    rows = pl.pallas_call(
        solve_kernel,
        out_shape=jax.ShapeDtypeStruct((ROWS, 2 * FL), bf16),
        in_specs=[vmem] * 3,
        out_specs=vmem,
        scratch_shapes=[
            pltpu.VMEM((LEV, TILE_COLS), f32),
            pltpu.VMEM((LEV, NF, TILE_COLS), f32),
            pltpu.VMEM((FL, TILE_COLS), f32),
            pltpu.VMEM((TILE_COLS, 2 * FL), f32),
            pltpu.VMEM((ROWS, 2 * FL), f32),
        ],
        compiler_params=params,
        name="solve",
    )(column_state, diffusivity, tile_map)
    table, twiddle = pl.pallas_call(
        table_kernel,
        out_shape=[
            jax.ShapeDtypeStruct((2, HALF, 2 * LANES), bf16),
            jax.ShapeDtypeStruct((4, 8, LANES), f32),
        ],
        in_specs=[smem, smem, smem, vmem],
        out_specs=[vmem, vmem],
        compiler_params=params,
        cost_estimate=pl.CostEstimate(flops=20_000_000, bytes_accessed=1_300_000, transcendentals=0),
        name="tables",
    )(row_len, lat_rows, pos, wave_order.reshape(8, OWN))
    rows = rows.reshape(SETS, CHUNK // 2, 2, 2 * FL)
    rows = lax.all_to_all(rows, ("z", "y"), split_axis=0, concat_axis=0, tiled=True)
    rows = rows.reshape(ROWS, 2 * FL)
    rows = lax.all_gather(rows, "x", axis=0, tiled=False)
    half = jax.ShapeDtypeStruct((2, 2, FL, OWN), f32)
    own, theirs = pl.pallas_call(
        transform_kernel,
        out_shape=[half, half],
        in_specs=[smem, smem, smem, vmem, vmem, vmem],
        out_specs=[vmem, vmem],
        compiler_params=params,
        name="transform",
    )(row_len, lat_rows, pos, rows, table, twiddle)
    got = lax.ppermute(theirs, "core", [(0, 1), (1, 0)])
    return pl.pallas_call(
        add_kernel,
        out_shape=jax.ShapeDtypeStruct((2, FL, 2, OWN), f32),
        in_specs=[vmem, vmem],
        out_specs=vmem,
        compiler_params=params,
        name="add",
    )(own, got)


def solution(mesh):
    chips = Mesh(mesh.devices.reshape(16, 4, 4, 2), ("z", "y", "x", "core"))
    columns = ("z", "y", "x", "core")
    return jax.shard_map(
        body,
        mesh=chips,
        in_specs=(
            P(None, None, columns),
            P(None, columns),
            P(),
            P(("z", "y")),
            P(),
            P(columns, None),
        ),
        out_specs=P(None, None, ("z", "y"), ("x", "core")),
        check_vma=False,
    )
```

time: 216 us -> 65.5 us (0.30)
  other arithmetic: 110 us -> 0 us
  matrix products: 28.5 us -> 0 us
  local copies, waits for them, and re-layouts: 32.5 us -> 4.65 us
  waiting for transfers between devices: 0.57 us -> 14.1 us
  Pallas kernels: 0 us -> 7.11 us
  between operations: 5.82 us -> 0.04 us
  starting transfers between devices: 24.5 us -> 28.1 us
  loops' own time: 2.39 us -> 0 us
    another operation x2 -> x0, other arithmetic: 71.7 us -> none
    dot_general x21 -> x0, matrix products: 28.5 us -> none  [add_block(): jnp.dot(slab_values, base_table, preferred_element_type=jnp.float32)]
    lt x21 -> x0, other arithmetic: 14 us -> none  [add_block(): inside = first_slot + positions < length]
    dynamic_update_slice x32 -> x0, other arithmetic: 12.7 us -> none  [vertical_solve(): lax.scan(forward, start_pair, (below_coef, above_coef, column_state))]
    all_to_all x2 -> x1, waiting for transfers between devices: 0.57 us -> 13 us  [body(): lax.all_to_all(rows, ('z', 'y'), split_axis=0, concat_axis=0, tiled=True)]
    all_gather x0 -> x1, blocking collectives: none -> 11.1 us  [body(): rows = lax.all_gather(rows, 'x', axis=0, tiled=False)]
    unnamed x14, local copies, waits for them, and re-layouts: 13.7 us -> 3.88 us
    all_to_all x1 -> x0, blocking collectives: 9.63 us -> none  [body(): lax.all_to_all(spectra, 'narrow', split_axis=3, concat_axis=1, tiled=True)]
  transfers between devices with their start and end apart: 2 -> 2, of which waited for: 1 -> 2; matrix products, arithmetic and copies ran while one was open for 36% -> 1% of each run, Pallas kernels for 0% -> 3%
where the time goes in v1:
time: 65.5 us; the launch traced here: 65.1 us
  starting transfers between devices  28.1 us (43%)
  waiting for transfers between devices  14.1 us (22%)
  blocking collectives  11.1 us (17%)
  Pallas kernels  7.11 us (11%)
  local copies, waits for them, and re-layouts  4.65 us (7%)
    all_to_all x1, starting transfers between devices, body(): lax.all_to_all(rows, ('z', 'y'), split_axis=0, concat_axis=0, tiled=True)  19.3 us
    all_to_all x1, waiting for transfers between devices, body(): lax.all_to_all(rows, ('z', 'y'), split_axis=0, concat_axis=0, tiled=True)  13 us
    all_gather x1, blocking collectives, body(): rows = lax.all_gather(rows, 'x', axis=0, tiled=False)  11.1 us
    ppermute x1, starting transfers between devices, body(): got = lax.ppermute(theirs, 'core', [(0, 1), (1, 0)])  8.78 us
    unnamed x14, local copies, waits for them, and re-layouts  3.88 us
    pallas_call x1, Pallas kernels, body(): pl.pallas_call(solve_kernel, out_shape=jax.ShapeDtypeStruct((ROWS, 2 * FL...  2.35 us
    pallas_call x1, Pallas kernels, body(): pl.pallas_call(table_kernel, out_shape=[jax.ShapeDtypeStruct((2, HALF, 2...  2.11 us
    pallas_call x1, Pallas kernels, body(): pl.pallas_call(transform_kernel, out_shape=[half, half], in_specs=[smem,...  1.85 us
  transfers between devices with their start and end apart: 2, of which 2 were waited for; matrix products, arithmetic and copies ran while one was open for 1% of the time, Pallas kernels for 3%

profile of v1, /device:TPU:1, one launch (start us, length us, event | category | flops | bytes accessed | tf_op | source)
XLA Modules:
  0.0 65.1 jit_solution(9408755511764835235)
XLA Ops:
  0.0 0.0 copy-start
  0.0 1.0 %copy-done = f32[16,4,1408]{2,1,0:T(4,128)S(1)} copy-done((f32[16,4,1408]{2,1,0:T(4,128)S(1)}, f32[16,4,1408]{2,1,0:T(4,128)}, u32[]{:S(2)}) %copy-start) | copy-done | bytes 360472
  1.0 0.0 copy-start.1
  1.0 0.9 %copy-done.1 = f32[15,1408]{1,0:T(8,128)S(1)} copy-done((f32[15,1408]{1,0:T(8,128)S(1)}, f32[15,1408]{1,0:T(8,128)}, u32[]{:S(2)}) %copy-start.1) | copy-done | bytes 84504
  1.9 0.0 copy-start.2
  1.9 0.7 %copy-done.2 = s32[1,1408]{1,0:T(1,128)S(1)} copy-done((s32[1,1408]{1,0:T(1,128)S(1)}, s32[1,1408]{1,0:T(1,128)}, u32[]{:S(2)}) %copy-start.2) | copy-done | bytes 5656
  2.6 0.0 copy-start.4
  2.6 0.0 copy-start.6
  2.6 2.3 %solve.1 = bf16[768,128]{1,0:T(8,128)(2,1)} custom-call(f32[16,4,1408]{2,1,0:T(4,128)S(1)} %copy-done, f32[15,1408]{1,0:T(8,128)S(1)} %copy-done.1, s32[1,1408]{1,0:T(1,128)S(1)} %copy-done.2), custom_call_target="tpu_custom_call" | custom-call | tf_op jit(solution)/shard_map/solve/pallas_call | solution.py:153
  4.9 19.3 %all-to-all-start = ((bf16[64,6,2,128]{3,2,1,0:T(2,128)(2,1)}), bf16[64,6,2,128]{3,2,1,0:T(2,128)(2,1)S(1)}, u32[]{:S(2)}, u32[]{:S(2)}) async-start(bf16[64,6,2,128]{3,2,1,0:T(2,128)(2,1)} %bitcast.1), calls=%async_computation | async-start | bytes 393216 | tf_op jit(solution)/shard_map/all_to_all | solution.py:181
  24.2 0.8 %reshape.11.wave_ref = s32[8,160]{1,0:T(8,128)S(1)} reshape(s32[1280]{0:T(1024)} %param.10) | data formatting | bytes 10240 | tf_op jit(solution)/shard_map/reshape | solution.py:179
  25.0 0.0 copy-start.3
  25.0 0.7 %copy-done.3 = s32[128]{0:T(128)S(1)} copy-done((s32[128]{0:T(128)S(1)}, s32[128]{0:T(128)}, u32[]{:S(2)}) %copy-start.3) | copy-done | bytes 536
  25.6 0.0 copy-start.5
  25.6 0.7 %copy-done.5 = s32[2]{0:T(128)S(1)} copy-done((s32[2]{0:T(128)S(1)}, s32[2]{0:T(128)}, u32[]{:S(2)}) %copy-start.5) | copy-done | bytes 32
  26.3 2.1 %tables.1 = (bf16[2,384,768]{2,1,0:T(8,128)(2,1)S(1)}, f32[4,8,384]{2,1,0:T(8,128)S(1)}) custom-call(s32[128]{0:T(128)S(1)} %copy-done.3, s32[2]{0:T(128)S(1)} %copy-done.5, s32[1]{0:T(128)} %bitcast.pos_ref, s32[8,160]{1,0:T(8,128)S(1)} %reshape.11.wave_ref), custom_call_target="tpu_custom_call" | custom-call | flops 20000000 | bytes 1300000 | tf_op jit(solution)/shard_map/tables/pallas_call | solution.py:168
  28.4 13.0 %all-to-all-done = bf16[64,6,2,128]{3,2,1,0:T(2,128)(2,1)S(1)} async-done(((bf16[64,6,2,128]{3,2,1,0:T(2,128)(2,1)}), bf16[64,6,2,128]{3,2,1,0:T(2,128)(2,1)S(1)}, u32[]{:S(2)}, u32[]{:S(2)}) %all-to-all-start) | async-done | bytes 196640 | tf_op jit(solution)/shard_map/all_to_all | solution.py:181
  41.4 11.1 %all_gather.3.rows_ref = bf16[4,768,128]{2,1,0:T(8,128)(2,1)S(1)} all-gather(bf16[1,768,128]{2,1,0:T(8,128)(2,1)S(1)} %bitcast.3), channel_id=1, replica_groups=mesh['z'=16,'y'=4,'x'=4,'core'=2] {'x'}, dimensions={0}, use_global_device_ids=true | all-gather | bytes 983040 | tf_op jit(solution)/shard_map/all_gather | solution.py:183
  52.5 0.0 copy-done.4
  52.5 0.0 copy-done.6
  52.5 1.9 %transform.1 = (f32[2,2,64,160]{3,2,1,0:T(8,128)S(1)}, f32[2,2,64,160]{3,2,1,0:T(8,128)S(1)}) custom-call(s32[128]{0:T(128)S(1)} %copy-done.4, s32[2]{0:T(128)S(1)} %copy-done.6, s32[1]{0:T(128)} %bitcast.pos_ref, bf16[4,768,128]{2,1,0:T(8,128)(2,1)S(1)} %all_gather.3.rows_ref, bf16[2,384,768]{2,1,0:T(8,128)(2,1)S(1)} %get-tuple-element.9.table_ref, ...), custom_call_target="tpu_custom_call" | custom-call | tf_op jit(solution)/shard_map/transform/pallas_call | solution.py:185
  54.4 8.8 %collective-permute-start = (f32[2,2,64,160]{3,2,1,0:T(8,128)S(1)}, f32[2,2,64,160]{3,2,1,0:T(8,128)S(1)}, u32[]{:S(2)}, u32[]{:S(2)}) collective-permute-start(f32[2,2,64,160]{3,2,1,0:T(8,128)S(1)} %get-tuple-element.12), channel_id=1, source_target_pairs={{0,1},{1,0},{2,3},{3,2},{4,5},{5,4},{6,7},{7,6},{8,9},{9,8},{10,11... | collective-permute-start | bytes 491528 | tf_op jit(solution)/shard_map/ppermute | solution.py:193
  63.2 1.1 %collective-permute-done.got_ref = f32[2,2,64,160]{3,2,1,0:T(8,128)S(1)} collective-permute-done((f32[2,2,64,160]{3,2,1,0:T(8,128)S(1)}, f32[2,2,64,160]{3,2,1,0:T(8,128)S(1)}, u32[]{:S(2)}, u32[]{:S(2)}) %collective-permute-start) | collective-permute-done | bytes 163872 | tf_op jit(solution)/shard_map/ppermute | solution.py:193
  64.3 0.8 %add.5 = f32[2,64,2,160]{3,2,1,0:T(2,128)} custom-call(f32[2,2,64,160]{3,2,1,0:T(8,128)S(1)} %get-tuple-element.11.own_ref, f32[2,2,64,160]{3,2,1,0:T(8,128)S(1)} %collective-permute-done.got_ref), custom_call_target="tpu_custom_call" | custom-call | tf_op jit(solution)/shard_map/add/pallas_call | solution.py:194
Async XLA Ops:
  0.0 1.0 %copy-start = (f32[16,4,1408]{2,1,0:T(4,128)S(1)}, f32[16,4,1408]{2,1,0:T(4,128)}, u32[]{:S(2)}) copy-start(f32[16,4,1408]{2,1,0:T(4,128)} %state_ref.1) | copy-start | bytes 1081348
  1.0 0.9 %copy-start.1 = (f32[15,1408]{1,0:T(8,128)S(1)}, f32[15,1408]{1,0:T(8,128)}, u32[]{:S(2)}) copy-start(f32[15,1408]{1,0:T(8,128)} %diff_ref.1) | copy-start | bytes 253444
  1.9 0.7 %copy-start.2 = (s32[1,1408]{1,0:T(1,128)S(1)}, s32[1,1408]{1,0:T(1,128)}, u32[]{:S(2)}) copy-start(s32[1,1408]{1,0:T(1,128)} %map_ref.1) | copy-start | bytes 16900
  2.6 50.0 %copy-start.4 = (s32[128]{0:T(128)S(1)}, s32[128]{0:T(128)}, u32[]{:S(2)}) copy-start(s32[128]{0:T(128)} %len_ref.3) | copy-start | bytes 1540
  2.6 50.0 %copy-start.6 = (s32[2]{0:T(128)S(1)}, s32[2]{0:T(128)}, u32[]{:S(2)}) copy-start(s32[2]{0:T(128)} %lat_ref.3) | copy-start | bytes 28
  4.9 36.5 %all-to-all-start = ((bf16[64,6,2,128]{3,2,1,0:T(2,128)(2,1)}), bf16[64,6,2,128]{3,2,1,0:T(2,128)(2,1)S(1)}, u32[]{:S(2)}, u32[]{:S(2)}) async-start(bf16[64,6,2,128]{3,2,1,0:T(2,128)(2,1)} %bitcast.1), calls=%async_computation | async-start | bytes 393216 | tf_op jit(solution)/shard_map/all_to_all | solution.py:181
  25.0 0.7 %copy-start.3 = (s32[128]{0:T(128)S(1)}, s32[128]{0:T(128)}, u32[]{:S(2)}) copy-start(s32[128]{0:T(128)} %len_ref.3) | copy-start | bytes 1540
  25.6 0.7 %copy-start.5 = (s32[2]{0:T(128)S(1)}, s32[2]{0:T(128)}, u32[]{:S(2)}) copy-start(s32[2]{0:T(128)} %lat_ref.3) | copy-start | bytes 28
  54.4 9.9 %collective-permute-start = (f32[2,2,64,160]{3,2,1,0:T(8,128)S(1)}, f32[2,2,64,160]{3,2,1,0:T(8,128)S(1)}, u32[]{:S(2)}, u32[]{:S(2)}) collective-permute-start(f32[2,2,64,160]{3,2,1,0:T(8,128)S(1)} %get-tuple-element.12), channel_id=1, source_target_pairs={{0,1},{1,0},{2,3},{3,2},{4,5},{5,4},{6,7},{7,6},{8,9},{9,8},{10,11... | collective-permute-start | bytes 491528 | tf_op jit(solution)/shard_map/ppermute | solution.py:193

commit v2 on v1

v2 whole, which is shorter than its diff:
```python
import math

import jax
import jax.numpy as jnp
from jax import lax
from jax.experimental import pallas as pl
from jax.experimental.pallas import tpu as pltpu
from jax.sharding import Mesh, PartitionSpec as P

LEV = 16
NF = 4
FL = 64
SETS = 64
PIECE = 22
TILE_COLS = 1408
CHUNK = 12
ROWS = SETS * CHUNK
HALF = ROWS // 2
BASE = HALF // 2
OWN = 160
MAIN = 128
TAIL = OWN - MAIN
PEERS = 8
CHIPS = 4
MODES = PEERS * OWN
SHARE = CHIPS * OWN
VMEM = 40 * 1024 * 1024
SOLVE_VMEM = 62 * 1024 * 1024


def solve_kernel(state_hbm, diff_hbm, map_hbm, out_ref, state_ref, diff_ref, map_ref, ratio_ref, value_ref, cols_ref, pick_ref, slots_ref, rows_ref, sems):
    copies = [pltpu.make_async_copy(map_hbm, map_ref, sems.at[0]), pltpu.make_async_copy(diff_hbm, diff_ref, sems.at[1])]
    for part in range(4):
        levels = pl.ds(4 * part, 4)
        copies.append(pltpu.make_async_copy(state_hbm.at[levels], state_ref.at[levels], sems.at[2 + part]))
    for copy in copies:
        copy.start()
    copies[0].wait()
    for first in range(0, TILE_COLS, 128):
        ids = lax.broadcasted_iota(jnp.int32, (TILE_COLS, 128), 0)
        pick = jnp.where(ids == map_ref[0:1, first : first + 128], 1.0, 0.0)
        pick_ref[:, first : first + 128] = pick.astype(jnp.bfloat16)
    copies[1].wait()
    ratio = jnp.zeros((1, TILE_COLS), jnp.float32)
    value = jnp.zeros((NF, TILE_COLS), jnp.float32)
    below = jnp.zeros((1, TILE_COLS), jnp.float32)
    for lev in range(LEV):
        if lev % 4 == 0:
            copies[2 + lev // 4].wait()
        if lev < LEV - 1:
            above = diff_ref[lev : lev + 1, :]
        else:
            above = jnp.zeros((1, TILE_COLS), jnp.float32)
        inverse = 1.0 / (1.0 + below + above + below * ratio)
        ratio = -above * inverse
        value = (state_ref[lev] + below * value) * inverse
        ratio_ref[lev : lev + 1, :] = ratio
        value_ref[lev] = value
        below = above
    solved = value
    cols_ref[(LEV - 1) * NF : LEV * NF, :] = solved
    for lev in range(LEV - 2, -1, -1):
        solved = value_ref[lev] - ratio_ref[lev : lev + 1, :] * solved
        cols_ref[lev * NF : (lev + 1) * NF, :] = solved
    cols = cols_ref[...].astype(jnp.bfloat16)
    cols = jnp.concatenate([cols, cols], axis=0)
    step = 256
    for first in range(0, TILE_COLS, step):
        width = min(step, TILE_COLS - first)
        moved = jnp.dot(cols, pick_ref[:, first : first + width], preferred_element_type=jnp.float32)
        slots_ref[first : first + width, :] = moved.T
    low_lane = lax.broadcasted_iota(jnp.int32, (PIECE // 2, 2 * FL), 1) < FL
    zero_row = jnp.zeros((1, 2 * FL), jnp.float32)
    for s in range(SETS):
        even = slots_ref[pl.ds(s * PIECE, PIECE // 2, stride=2), :]
        odd = slots_ref[pl.ds(s * PIECE + 1, PIECE // 2, stride=2), :]
        both = jnp.where(low_lane, even, odd)
        rows_ref[s * CHUNK : s * CHUNK + PIECE // 2, :] = both
        rows_ref[s * CHUNK + PIECE // 2 : (s + 1) * CHUNK, :] = zero_row
    out_ref[...] = rows_ref[...].astype(jnp.bfloat16)


def cos_sin_turns(turns):
    square = turns * turns
    s = jnp.full_like(turns, -(math.pi**11) / math.factorial(11))
    for k, sign in ((9, 1.0), (7, -1.0), (5, 1.0), (3, -1.0), (1, 1.0)):
        s = s * square + sign * math.pi**k / math.factorial(k)
    s = s * turns
    c = jnp.full_like(turns, (math.pi**12) / math.factorial(12))
    for k, sign in ((10, -1.0), (8, 1.0), (6, -1.0), (4, 1.0), (2, -1.0), (0, 1.0)):
        c = c * square + sign * math.pi**k / math.factorial(k)
    return 1.0 - 2.0 * s * s, 2.0 * s * c


def turns_of(product, length, inverse):
    return (product - jnp.floor(product * inverse + 0.5) * length) * inverse


def row_lengths(len_ref, lat_ref, r):
    return len_ref[lat_ref[r]]


def table_kernel(len_ref, lat_ref, pos_ref, wave_ref, table_ref, twiddle_ref, limit_ref):
    core = lax.rem(pos_ref[0], 2)
    waves = []
    for side in (core, 1 - core):
        rows_of = [wave_ref[pl.ds(2 * chip + side, 1), :] for chip in range(CHIPS)]
        waves += [row[:, 0:MAIN] for row in rows_of] + [row[:, MAIN:OWN] for row in rows_of]
    waves = jnp.concatenate(waves, axis=1).astype(jnp.float32)
    rows = 8
    for r in range(2):
        limit_ref[r] = jnp.full((8, 2 * FL), row_lengths(len_ref, lat_ref, r) - PIECE * pos_ref[0], jnp.int32)
        length = jnp.full((1, MODES), row_lengths(len_ref, lat_ref, r), jnp.int32).astype(jnp.float32)
        inverse = 1.0 / length
        scale = lax.rsqrt(length)
        scale = scale * (1.5 - 0.5 * length * scale * scale)

        def some_rows(step, carry):
            first = pl.multiple_of(step * 2 * rows, 2 * rows)
            cosines, sines = [], []
            for part in range(2):
                row = lax.broadcasted_iota(jnp.int32, (rows, MODES), 0) + (first + part * rows)
                row = row.astype(jnp.float32)
                group = jnp.floor((row + 0.5) * (1.0 / CHUNK))
                slot = 8.0 * PIECE * group + 2.0 * (row - CHUNK * group)
                cosine, sine = cos_sin_turns(turns_of(slot * waves, length, inverse))
                cosines.append(cosine)
                sines.append(-sine)
            table_ref[r, pl.ds(first, 2 * rows), 0:MODES] = jnp.concatenate(cosines, axis=0).astype(jnp.bfloat16)
            table_ref[r, pl.ds(first, 2 * rows), MODES:] = jnp.concatenate(sines, axis=0).astype(jnp.bfloat16)
            return carry

        lax.fori_loop(0, BASE // (2 * rows), some_rows, 0)
        item = lax.broadcasted_iota(jnp.int32, (8, MODES), 0)
        shift = (BASE // CHUNK) * 8 * PIECE * (item // 2) + item % 2 + PIECE * pos_ref[0]
        cosine, sine = cos_sin_turns(turns_of(shift.astype(jnp.float32) * waves, length, inverse))
        twiddle_ref[2 * r] = cosine * scale
        twiddle_ref[2 * r + 1] = sine * scale


def combine(values, table_ref, twiddle_ref, r, first, width):
    lanes = slice(first, first + width)
    cos_all = jnp.dot(values, table_ref[r, :, lanes], preferred_element_type=jnp.float32)
    sin_lanes = slice(MODES + first, MODES + first + width)
    sin_all = jnp.dot(values, table_ref[r, :, sin_lanes], preferred_element_type=jnp.float32)
    real = jnp.zeros((FL, width), jnp.float32)
    imag = jnp.zeros((FL, width), jnp.float32)
    for item in range(4):
        cos_part = cos_all[item * FL : (item + 1) * FL]
        sin_part = sin_all[item * FL : (item + 1) * FL]
        tc = twiddle_ref[2 * r, item : item + 1, lanes]
        ts = twiddle_ref[2 * r + 1, item : item + 1, lanes]
        real = real + tc * cos_part + ts * sin_part
        imag = imag + tc * sin_part - ts * cos_part
    return real, imag


def share_of(values_of, start, table_ref, twiddle_ref, out_ref, tails_ref):
    for r in range(2):
        values = values_of(r)
        for pair in range(CHIPS // 2):
            sums = combine(values, table_ref, twiddle_ref, r, start + 2 * MAIN * pair, 2 * MAIN)
            for part in range(2):
                k = 2 * part + r
                for half in range(2):
                    block = sums[part][:, half * MAIN : (half + 1) * MAIN]
                    out_ref[2 * pair + half, k * FL : (k + 1) * FL, :] = block.astype(out_ref.dtype)
        sums = combine(values, table_ref, twiddle_ref, r, start + CHIPS * MAIN, CHIPS * TAIL)
        for part in range(2):
            tails_ref[2 * part + r] = sums[part]
    for chip in range(CHIPS):
        tail = [tails_ref[k, :, TAIL * chip : TAIL * (chip + 1)] for k in range(4)]
        out_ref[chip, 4 * FL :, :] = jnp.concatenate(tail, axis=1).astype(out_ref.dtype)


def other_kernel(rows_ref, limit_ref, table_ref, twiddle_ref, out_ref, values_ref, tails_ref):
    row = lax.broadcasted_iota(jnp.int32, (HALF, 2 * FL), 0)
    lane = lax.broadcasted_iota(jnp.int32, (HALF, 2 * FL), 1)
    group = row // CHUNK
    inner = row - CHUNK * group
    slot = 8 * PIECE * group + 2 * inner + jnp.where(lane >= FL, 1, 0)
    slot = jnp.where(inner == CHUNK - 1, 1 << 20, slot)

    def values_of(r):
        inside = slot < limit_ref[r, 0:1, :]
        values = jnp.where(inside, rows_ref[r * HALF : (r + 1) * HALF, :].astype(jnp.float32), 0.0)
        values = jnp.concatenate([values[:BASE].T, values[BASE:].T], axis=0).astype(jnp.bfloat16)
        values_ref[r] = values
        return values

    share_of(values_of, SHARE, table_ref, twiddle_ref, out_ref, tails_ref)


def own_kernel(values_ref, table_ref, twiddle_ref, out_ref, tails_ref):
    share_of(lambda r: values_ref[r], 0, table_ref, twiddle_ref, out_ref, tails_ref)


def pair_kernel(own_ref, got_ref, out_ref):
    for chip in range(CHIPS):
        out_ref[chip] = (own_ref[chip] + got_ref[chip].astype(jnp.float32)).astype(jnp.bfloat16)


def add_kernel(got_ref, out_ref):
    def total(start, stop):
        sums = got_ref[0, start:stop, :].astype(jnp.float32)
        for chip in range(1, CHIPS):
            sums = sums + got_ref[chip, start:stop, :].astype(jnp.float32)
        return sums

    tail = total(4 * FL, 5 * FL)
    for part in range(2):
        for r in range(2):
            k = 2 * part + r
            main = total(k * FL, (k + 1) * FL)
            both = jnp.concatenate([main, tail[:, k * TAIL : (k + 1) * TAIL]], axis=1)
            out_ref[part, :, r, :] = both


def body(column_state, diffusivity, row_len, lat_rows, wave_order, tile_map):
    f32, bf16 = jnp.float32, jnp.bfloat16
    pos = (2 * lax.axis_index("x") + lax.axis_index("core")).astype(jnp.int32).reshape(1)
    smem = pl.BlockSpec(memory_space=pltpu.SMEM)
    vmem = pl.BlockSpec(memory_space=pltpu.VMEM)
    hbm = pl.BlockSpec(memory_space=pltpu.HBM)
    params = pltpu.CompilerParams(vmem_limit_bytes=VMEM)
    rows = pl.pallas_call(
        solve_kernel,
        out_shape=jax.ShapeDtypeStruct((ROWS, 2 * FL), bf16),
        in_specs=[hbm] * 3,
        out_specs=vmem,
        scratch_shapes=[
            pltpu.VMEM((LEV, NF, TILE_COLS), f32),
            pltpu.VMEM((LEV - 1, TILE_COLS), f32),
            pltpu.VMEM((1, TILE_COLS), jnp.int32),
            pltpu.VMEM((LEV, TILE_COLS), f32),
            pltpu.VMEM((LEV, NF, TILE_COLS), f32),
            pltpu.VMEM((FL, TILE_COLS), f32),
            pltpu.VMEM((TILE_COLS, TILE_COLS), bf16),
            pltpu.VMEM((TILE_COLS, 2 * FL), f32),
            pltpu.VMEM((ROWS, 2 * FL), f32),
            pltpu.SemaphoreType.DMA((6,)),
        ],
        compiler_params=pltpu.CompilerParams(vmem_limit_bytes=SOLVE_VMEM),
        name="solve",
    )(column_state, diffusivity, tile_map)
    table, twiddle, limit = pl.pallas_call(
        table_kernel,
        out_shape=[
            jax.ShapeDtypeStruct((2, BASE, 2 * MODES), bf16),
            jax.ShapeDtypeStruct((4, 8, MODES), f32),
            jax.ShapeDtypeStruct((2, 8, 2 * FL), jnp.int32),
        ],
        in_specs=[smem, smem, smem, vmem],
        out_specs=[vmem, vmem, vmem],
        compiler_params=params,
        cost_estimate=pl.CostEstimate(flops=40_000_000, bytes_accessed=2_200_000, transcendentals=0),
        name="tables",
    )(row_len, lat_rows, pos, wave_order.reshape(PEERS, OWN))
    rows = rows.reshape(SETS, CHUNK // 2, 2, 2 * FL)
    rows = lax.all_to_all(rows, ("z", "y"), split_axis=0, concat_axis=0, tiled=True)
    rows = rows.reshape(ROWS, 2 * FL)
    rows, table, twiddle, limit = lax.optimization_barrier((rows, table, twiddle, limit))
    tails = pltpu.VMEM((4, FL, CHIPS * TAIL), f32)
    other, values = pl.pallas_call(
        other_kernel,
        out_shape=[
            jax.ShapeDtypeStruct((CHIPS, 5 * FL, MAIN), bf16),
            jax.ShapeDtypeStruct((2, 4 * FL, BASE), bf16),
        ],
        in_specs=[vmem] * 4,
        out_specs=[vmem] * 2,
        scratch_shapes=[tails],
        compiler_params=params,
        name="transform_other",
    )(rows, limit, table, twiddle)
    got = lax.ppermute(other, "core", [(0, 1), (1, 0)])
    own = pl.pallas_call(
        own_kernel,
        out_shape=jax.ShapeDtypeStruct((CHIPS, 5 * FL, MAIN), f32),
        in_specs=[vmem] * 3,
        out_specs=vmem,
        scratch_shapes=[tails],
        compiler_params=params,
        cost_estimate=pl.CostEstimate(flops=500_000_000, bytes_accessed=2_000_000, transcendentals=0),
        name="transform_own",
    )(values, table, twiddle)
    sums = pl.pallas_call(
        pair_kernel,
        out_shape=jax.ShapeDtypeStruct((CHIPS, 5 * FL, MAIN), bf16),
        in_specs=[vmem] * 2,
        out_specs=vmem,
        compiler_params=params,
        name="pair",
    )(own, got)
    sums = lax.all_to_all(sums, "x", split_axis=0, concat_axis=0, tiled=True)
    return pl.pallas_call(
        add_kernel,
        out_shape=jax.ShapeDtypeStruct((2, FL, 2, OWN), f32),
        in_specs=[vmem],
        out_specs=vmem,
        compiler_params=params,
        name="add",
    )(sums)


def solution(mesh):
    chips = Mesh(mesh.devices.reshape(16, 4, 4, 2), ("z", "y", "x", "core"))
    columns = ("z", "y", "x", "core")
    return jax.shard_map(
        body,
        mesh=chips,
        in_specs=(
            P(None, None, columns),
            P(None, columns),
            P(),
            P(("z", "y")),
            P(),
            P(columns, None),
        ),
        out_specs=P(None, None, ("z", "y"), ("x", "core")),
        check_vma=False,
    )
```

time: 65.5 us -> 59.9 us (0.915)
  starting transfers between devices: 28.1 us -> 25.1 us
  local copies, waits for them, and re-layouts: 4.65 us -> 2.08 us
  Pallas kernels: 7.11 us -> 9.58 us
  waiting for transfers between devices: 14.1 us -> 12.1 us
    all_gather x1 -> x0, blocking collectives: 11.1 us -> none  [body(): rows = lax.all_gather(rows, 'x', axis=0, tiled=False)]
    all_to_all x0 -> x1, blocking collectives: none -> 10.6 us  [body(): sums = lax.all_to_all(sums, 'x', split_axis=0, concat_axis=0, tiled=True)]
    ppermute x1, starting transfers between devices: 8.78 us -> 5.85 us  [body(): got = lax.ppermute(other, 'core', [(0, 1), (1, 0)])]
    unnamed x14 -> x4, local copies, waits for them, and re-layouts: 3.88 us -> 1.31 us
    all_to_all x1, waiting for transfers between devices: 13 us -> 11.6 us  [body(): lax.all_to_all(rows, ('z', 'y'), split_axis=0, concat_axis=0, tiled=True)]
    pallas_call x1, Pallas kernels: 2.35 us -> 3.69 us  [body(): pl.pallas_call(solve_kernel, out_shape=jax.ShapeDtypeStruct((ROWS, 2 * FL...]
    pallas_call x2 -> x4, Pallas kernels: 3.96 us -> 5.05 us  [the longest x1 3.53 us: body(): pl.pallas_call(table_kernel, out_shape=[jax.ShapeDtypeStruct((2, BASE, 2...]
  transfers between devices with their start and end apart: 2 -> 2, of which waited for: 2 -> 2; matrix products, arithmetic and copies ran while one was open for 1% -> 1% of each run, Pallas kernels for 3% -> 7%
where the time goes in v2:
time: 59.9 us; the launch traced here: 59.6 us
  starting transfers between devices  25.1 us (42%)
  waiting for transfers between devices  12.1 us (20%)
  blocking collectives  10.6 us (18%)
  Pallas kernels  9.58 us (16%)
  local copies, waits for them, and re-layouts  2.08 us (3%)
    all_to_all x1, starting transfers between devices, body(): lax.all_to_all(rows, ('z', 'y'), split_axis=0, concat_axis=0, tiled=True)  19.3 us
    all_to_all x1, waiting for transfers between devices, body(): lax.all_to_all(rows, ('z', 'y'), split_axis=0, concat_axis=0, tiled=True)  11.6 us
    all_to_all x1, blocking collectives, body(): sums = lax.all_to_all(sums, 'x', split_axis=0, concat_axis=0, tiled=True)  10.6 us
    ppermute x1, starting transfers between devices, body(): got = lax.ppermute(other, 'core', [(0, 1), (1, 0)])  5.85 us
    pallas_call x1, Pallas kernels, body(): pl.pallas_call(solve_kernel, out_shape=jax.ShapeDtypeStruct((ROWS, 2 * FL...  3.69 us
    pallas_call x1, Pallas kernels, body(): pl.pallas_call(table_kernel, out_shape=[jax.ShapeDtypeStruct((2, BASE, 2...  3.53 us
    unnamed x4, local copies, waits for them, and re-layouts  1.31 us
  transfers between devices with their start and end apart: 2, of which 2 were waited for; matrix products, arithmetic and copies ran while one was open for 1% of the time, Pallas kernels for 7%

profile of v2, /device:TPU:1, one launch (start us, length us, event | category | flops | bytes accessed | tf_op | source)
XLA Modules:
  0.0 59.6 jit_solution(11201132510111796810)
XLA Ops:
  0.0 3.7 %solve.1 = bf16[768,128]{1,0:T(8,128)(2,1)} custom-call(f32[16,4,1408]{2,1,0:T(4,128)} %state_hbm.1, f32[15,1408]{1,0:T(8,128)} %diff_hbm.1, s32[1,1408]{1,0:T(1,128)} %map_hbm.1), custom_call_target="tpu_custom_call" | custom-call | tf_op jit(solution)/shard_map/solve/pallas_call | solution.py:226
  3.7 19.3 %all-to-all-start = ((bf16[64,6,2,128]{3,2,1,0:T(2,128)(2,1)}), bf16[64,6,2,128]{3,2,1,0:T(2,128)(2,1)S(1)}, u32[]{:S(2)}, u32[]{:S(2)}) async-start(bf16[64,6,2,128]{3,2,1,0:T(2,128)(2,1)} %bitcast.4), calls=%async_computation | async-start | bytes 393216 | tf_op jit(solution)/shard_map/all_to_all | solution.py:260
  23.0 0.8 %reshape.15.wave_ref = s32[8,160]{1,0:T(8,128)S(1)} reshape(s32[1280]{0:T(1024)} %param.10) | data formatting | bytes 10240 | tf_op jit(solution)/shard_map/reshape | solution.py:258
  23.8 0.0 copy-start
  23.8 0.7 %copy-done = s32[128]{0:T(128)S(1)} copy-done((s32[128]{0:T(128)S(1)}, s32[128]{0:T(128)}, u32[]{:S(2)}) %copy-start) | copy-done | bytes 536
  24.4 0.0 copy-start.1
  24.4 0.7 %copy-done.1 = s32[2]{0:T(128)S(1)} copy-done((s32[2]{0:T(128)S(1)}, s32[2]{0:T(128)}, u32[]{:S(2)}) %copy-start.1) | copy-done | bytes 32
  25.1 3.5 %tables.1 = (bf16[2,192,2560]{2,1,0:T(8,128)(2,1)S(1)}, f32[4,8,1280]{2,1,0:T(8,128)S(1)}, s32[2,8,128]{2,1,0:T(8,128)S(1)}) custom-call(s32[128]{0:T(128)S(1)} %copy-done, s32[2]{0:T(128)S(1)} %copy-done.1, s32[1]{0:T(128)} %bitcast.2.pos_ref, s32[8,160]{1,0:T(8,128)S(1)} %reshape.15.wave_ref), custom_call_target="tpu_custom_call" | custom-call | flops 40000000 | bytes 2200000 | tf_op jit(solution)/shard_map/tables/pallas_call | solution.py:246
  28.6 11.6 %all-to-all-done = bf16[64,6,2,128]{3,2,1,0:T(2,128)(2,1)S(1)} async-done(((bf16[64,6,2,128]{3,2,1,0:T(2,128)(2,1)}), bf16[64,6,2,128]{3,2,1,0:T(2,128)(2,1)S(1)}, u32[]{:S(2)}, u32[]{:S(2)}) %all-to-all-start) | async-done | bytes 196640 | tf_op jit(solution)/shard_map/all_to_all | solution.py:260
  40.2 0.8 %transform_other.1 = (bf16[4,320,128]{2,1,0:T(8,128)(2,1)S(1)}, bf16[2,256,192]{2,1,0:T(8,128)(2,1)S(1)}) custom-call(bf16[768,128]{1,0:T(8,128)(2,1)S(1)} %bitcast.3, s32[2,8,128]{2,1,0:T(8,128)S(1)} %get-tuple-element.18.limit_ref, bf16[2,192,2560]{2,1,0:T(8,128)(2,1)S(1)} %get-tuple-element.19.table_ref, f32[4,8,1280]{2,1,0:T(8,128)S(1)} %get-tuple-element.20.twiddle_ref), custom_call_target="tpu_custom_call" | custom-call | tf_op jit(solution)/shard_map/transform_other/pallas_call | solution.py:264
  41.0 5.8 %collective-permute-start = (bf16[4,320,128]{2,1,0:T(8,128)(2,1)S(1)}, bf16[4,320,128]{2,1,0:T(8,128)(2,1)S(1)}, u32[]{:S(2)}, u32[]{:S(2)}) collective-permute-start(bf16[4,320,128]{2,1,0:T(8,128)(2,1)S(1)} %get-tuple-element.22), channel_id=1, source_target_pairs={{0,1},{1,0},{2,3},{3,2},{4,5},{5,4},{6,7},{7,6},{8,9},{9,8},{10,11... | collective-permute-start | bytes 983048 | tf_op jit(solution)/shard_map/ppermute | solution.py:276
  46.9 0.7 %transform_own.1.own_ref = f32[4,320,128]{2,1,0:T(8,128)S(1)} custom-call(bf16[2,256,192]{2,1,0:T(8,128)(2,1)S(1)} %get-tuple-element.21.values_ref, bf16[2,192,2560]{2,1,0:T(8,128)(2,1)S(1)} %get-tuple-element.19.table_ref, f32[4,8,1280]{2,1,0:T(8,128)S(1)} %get-tuple-element.20.twiddle_ref), custom_call_target="tpu_custom_call" | custom-call | flops 500000000 | bytes 2000000 | tf_op jit(solution)/shard_map/transform_own/pallas_call | solution.py:277
  47.5 0.6 collective-permute-done.got_ref
  48.1 0.1 pair.1
  48.2 10.6 %all_to_all.10.got_ref = bf16[4,320,128]{2,1,0:T(8,128)(2,1)S(1)} all-to-all(bf16[4,320,128]{2,1,0:T(8,128)(2,1)S(1)} %pair.1), channel_id=1, replica_groups=mesh['z'=16,'y'=4,'x'=4,'core'=2] {'x'}, dimensions={0} | all-to-all | bytes 655360 | tf_op jit(solution)/shard_map/all_to_all | solution.py:295
  58.8 0.8 %add.5 = f32[2,64,2,160]{3,2,1,0:T(2,128)} custom-call(bf16[4,320,128]{2,1,0:T(8,128)(2,1)S(1)} %all_to_all.10.got_ref), custom_call_target="tpu_custom_call" | custom-call | tf_op jit(solution)/shard_map/add/pallas_call | solution.py:296
Async XLA Ops:
  3.7 36.5 %all-to-all-start = ((bf16[64,6,2,128]{3,2,1,0:T(2,128)(2,1)}), bf16[64,6,2,128]{3,2,1,0:T(2,128)(2,1)S(1)}, u32[]{:S(2)}, u32[]{:S(2)}) async-start(bf16[64,6,2,128]{3,2,1,0:T(2,128)(2,1)} %bitcast.4), calls=%async_computation | async-start | bytes 393216 | tf_op jit(solution)/shard_map/all_to_all | solution.py:260
  23.8 0.7 %copy-start = (s32[128]{0:T(128)S(1)}, s32[128]{0:T(128)}, u32[]{:S(2)}) copy-start(s32[128]{0:T(128)} %len_ref.1) | copy-start | bytes 1540
  24.4 0.7 %copy-start.1 = (s32[2]{0:T(128)S(1)}, s32[2]{0:T(128)}, u32[]{:S(2)}) copy-start(s32[2]{0:T(128)} %lat_ref.1) | copy-start | bytes 28
  41.0 7.1 %collective-permute-start = (bf16[4,320,128]{2,1,0:T(8,128)(2,1)S(1)}, bf16[4,320,128]{2,1,0:T(8,128)(2,1)S(1)}, u32[]{:S(2)}, u32[]{:S(2)}) collective-permute-start(bf16[4,320,128]{2,1,0:T(8,128)(2,1)S(1)} %get-tuple-element.22), channel_id=1, source_target_pairs={{0,1},{1,0},{2,3},{3,2},{4,5},{5,4},{6,7},{7,6},{8,9},{9,8},{10,11... | collective-permute-start | bytes 983048 | tf_op jit(solution)/shard_map/ppermute | solution.py:276

commit v3 on v2

v3 whole, which is shorter than its diff:
```python
import math

import jax
import jax.numpy as jnp
from jax import lax
from jax.experimental import pallas as pl
from jax.experimental.pallas import tpu as pltpu
from jax.sharding import Mesh, PartitionSpec as P

LEV = 16
NF = 4
FL = 64
SETS = 64
PIECE = 22
TILE_COLS = 1408
CHUNK = 12
ROWS = SETS * CHUNK
HALF = ROWS // 2
BASE = HALF // 2
OWN = 160
MAIN = 128
TAIL = OWN - MAIN
PEERS = 8
CHIPS = 4
ROW_TILES = 4
Z_ORDER = (0, 15, 1, 14, 2, 13, 3, 12, 4, 11, 5, 10, 6, 9, 7, 8)
ORDER = tuple(z * ROW_TILES + y for z in Z_ORDER for y in range(ROW_TILES))
SHARE = CHIPS * OWN
VMEM = 40 * 1024 * 1024
SOLVE_VMEM = 62 * 1024 * 1024


def lane_gather(values, lanes):
    return jnp.take_along_axis(values, lanes, axis=1, mode="promise_in_bounds")


def solve_kernel(state_hbm, diff_hbm, map_hbm, out_ref, state_ref, diff_ref, map_ref, ratio_ref, value_ref, cols_ref, pick_ref, rows_ref, sems):
    copies = [pltpu.make_async_copy(map_hbm, map_ref, sems.at[0]), pltpu.make_async_copy(diff_hbm, diff_ref, sems.at[1])]
    for part in range(4):
        levels = pl.ds(4 * part, 4)
        copies.append(pltpu.make_async_copy(state_hbm.at[levels], state_ref.at[levels], sems.at[2 + part]))
    for copy in copies:
        copy.start()
    copies[0].wait()
    tiles = ROWS // 128
    for part in range(2):
        for tile in range(tiles):
            place = (lax.broadcasted_iota(jnp.int32, (8, 128), 1) + 128 * tile).astype(jnp.float32)
            chunk = jnp.floor((place + 0.5) * (1.0 / CHUNK))
            inner = place - CHUNK * chunk
            slot = (PIECE * chunk + 2.0 * inner + part).astype(jnp.int32)
            lo_tile = (PIECE * (128 * tile // CHUNK)) // 128
            hi_tile = min(TILE_COLS // 128 - 1, (PIECE * ((128 * tile + 127) // CHUNK) + PIECE - 1) // 128)
            column = jnp.full((8, 128), -1, jnp.int32)
            for k in range(lo_tile, hi_tile + 1):
                entries = jnp.broadcast_to(map_ref[0:1, 128 * k : 128 * (k + 1)], (8, 128))
                found = lane_gather(entries, jnp.bitwise_and(slot, 127))
                column = jnp.where(slot // 128 == k, found, column)
            pick_ref[tiles * part + tile] = jnp.where(inner < PIECE // 2, column, -1)
    copies[1].wait()
    ratio = jnp.zeros((1, TILE_COLS), jnp.float32)
    value = jnp.zeros((NF, TILE_COLS), jnp.float32)
    below = jnp.zeros((1, TILE_COLS), jnp.float32)
    for lev in range(LEV):
        if lev % 4 == 0:
            copies[2 + lev // 4].wait()
        if lev < LEV - 1:
            above = diff_ref[lev : lev + 1, :]
        else:
            above = jnp.zeros((1, TILE_COLS), jnp.float32)
        inverse = 1.0 / (1.0 + below + above + below * ratio)
        ratio = -above * inverse
        value = (state_ref[lev] + below * value) * inverse
        ratio_ref[lev : lev + 1, :] = ratio
        value_ref[lev] = value
        below = above
    solved = value
    cols_ref[(LEV - 1) * NF : LEV * NF, :] = solved
    for lev in range(LEV - 2, -1, -1):
        solved = value_ref[lev] - ratio_ref[lev : lev + 1, :] * solved
        cols_ref[lev * NF : (lev + 1) * NF, :] = solved
    for tile in range(tiles):
        blocks = []
        for part in range(2):
            column = pick_ref[tiles * part + tile]
            lane = jnp.bitwise_and(column, 127)
            source = jnp.right_shift(column, 7)
            hits = [source == k for k in range(TILE_COLS // 128)]
            for first in range(0, FL, 8):
                block = jnp.zeros((8, 128), jnp.float32)
                for k in range(TILE_COLS // 128):
                    found = lane_gather(cols_ref[first : first + 8, 128 * k : 128 * (k + 1)], lane)
                    block = jnp.where(hits[k], found, block)
                blocks.append(block)
        rows_ref[128 * tile : 128 * (tile + 1), :] = jnp.concatenate(blocks, axis=0).T
    step = ROW_TILES * CHUNK
    for place, z in enumerate(Z_ORDER):
        block = rows_ref[step * z : step * (z + 1), :]
        out_ref[step * place : step * (place + 1), :] = block.astype(jnp.bfloat16)


def cos_sin_turns(turns):
    square = turns * turns
    s = jnp.full_like(turns, -(math.pi**11) / math.factorial(11))
    for k, sign in ((9, 1.0), (7, -1.0), (5, 1.0), (3, -1.0), (1, 1.0)):
        s = s * square + sign * math.pi**k / math.factorial(k)
    s = s * turns
    c = jnp.full_like(turns, (math.pi**12) / math.factorial(12))
    for k, sign in ((10, -1.0), (8, 1.0), (6, -1.0), (4, 1.0), (2, -1.0), (0, 1.0)):
        c = c * square + sign * math.pi**k / math.factorial(k)
    return 1.0 - 2.0 * s * s, 2.0 * s * c


def turns_of(product, length, inverse):
    return (product - jnp.floor(product * inverse + 0.5) * length) * inverse


def row_lengths(len_ref, lat_ref, r):
    return len_ref[lat_ref[r]]


def table_kernel(len_ref, lat_ref, pos_ref, wave_ref, table_ref, twiddle_ref, limit_ref):
    core = lax.rem(pos_ref[0], 2)
    rows_of = [wave_ref[pl.ds(2 * chip + core, 1), :] for chip in range(CHIPS)]
    waves = [row[:, 0:MAIN] for row in rows_of] + [row[:, MAIN:OWN] for row in rows_of]
    waves = jnp.concatenate(waves, axis=1).astype(jnp.float32)
    pieces = (pos_ref[0], pos_ref[0] + 1 - 2 * core)
    rows = 8
    for r in range(2):
        count = row_lengths(len_ref, lat_ref, r)
        for source in range(2):
            limit_ref[2 * source + r] = jnp.full((8, 2 * FL), count - PIECE * pieces[source], jnp.int32)
        length = jnp.full((1, SHARE), count, jnp.int32).astype(jnp.float32)
        inverse = 1.0 / length
        scale = lax.rsqrt(length)
        scale = scale * (1.5 - 0.5 * length * scale * scale)

        def some_rows(step, carry):
            first = pl.multiple_of(step * 2 * rows, 2 * rows)
            cosines, sines = [], []
            for part in range(2):
                row = lax.broadcasted_iota(jnp.int32, (rows, SHARE), 0) + (first + part * rows)
                row = row.astype(jnp.float32)
                group = jnp.floor((row + 0.5) * (1.0 / CHUNK))
                slot = 8.0 * PIECE * group + 2.0 * (row - CHUNK * group)
                cosine, sine = cos_sin_turns(turns_of(slot * waves, length, inverse))
                cosines.append(cosine)
                sines.append(-sine)
            table_ref[r, pl.ds(first, 2 * rows), 0:SHARE] = jnp.concatenate(cosines, axis=0).astype(jnp.bfloat16)
            table_ref[r, pl.ds(first, 2 * rows), SHARE:] = jnp.concatenate(sines, axis=0).astype(jnp.bfloat16)
            return carry

        lax.fori_loop(0, BASE // (2 * rows), some_rows, 0)
        item = lax.broadcasted_iota(jnp.int32, (8, SHARE), 0)
        shift = (BASE // CHUNK) * 8 * PIECE * (item // 2 % 2) + item % 2
        shift = shift + PIECE * jnp.where(item < 4, pieces[0], pieces[1])
        cosine, sine = cos_sin_turns(turns_of(shift.astype(jnp.float32) * waves, length, inverse))
        twiddle_ref[2 * r] = cosine * scale
        twiddle_ref[2 * r + 1] = sine * scale


def combine(values, table_ref, twiddle_ref, source, r, first, width):
    lanes = slice(first, first + width)
    cos_all = jnp.dot(values, table_ref[r, :, lanes], preferred_element_type=jnp.float32)
    sin_lanes = slice(SHARE + first, SHARE + first + width)
    sin_all = jnp.dot(values, table_ref[r, :, sin_lanes], preferred_element_type=jnp.float32)
    real = jnp.zeros((FL, width), jnp.float32)
    imag = jnp.zeros((FL, width), jnp.float32)
    for item in range(4):
        cos_part = cos_all[item * FL : (item + 1) * FL]
        sin_part = sin_all[item * FL : (item + 1) * FL]
        k = 4 * source + item
        tc = twiddle_ref[2 * r, k : k + 1, lanes]
        ts = twiddle_ref[2 * r + 1, k : k + 1, lanes]
        real = real + tc * cos_part + ts * sin_part
        imag = imag + tc * sin_part - ts * cos_part
    return real, imag


def transform(source, rows_ref, limit_ref, table_ref, twiddle_ref, store):
    row = lax.broadcasted_iota(jnp.int32, (HALF, 2 * FL), 0)
    lane = lax.broadcasted_iota(jnp.int32, (HALF, 2 * FL), 1)
    group = row // CHUNK
    inner = row - CHUNK * group
    slot = 8 * PIECE * group + 2 * inner + jnp.where(lane >= FL, 1, 0)
    slot = jnp.where(inner == CHUNK - 1, 1 << 20, slot)
    step = ROW_TILES * CHUNK
    tails = []
    for r in range(2):
        inside = slot < limit_ref[2 * source + r, 0:1, :]
        starts = [step * Z_ORDER.index(z) for z in range(r * len(Z_ORDER) // 2, (r + 1) * len(Z_ORDER) // 2)]
        values = jnp.concatenate([rows_ref[start : start + step, :] for start in starts], axis=0)
        values = jnp.where(inside, values.astype(jnp.float32), 0.0)
        values = jnp.concatenate([values[:BASE].T, values[BASE:].T], axis=0).astype(jnp.bfloat16)
        for pair in range(CHIPS // 2):
            sums = combine(values, table_ref, twiddle_ref, source, r, 2 * MAIN * pair, 2 * MAIN)
            for part in range(2):
                for half in range(2):
                    block = sums[part][:, half * MAIN : (half + 1) * MAIN]
                    store(2 * pair + half, (2 * part + r) * FL, block)
        tails.append(combine(values, table_ref, twiddle_ref, source, r, CHIPS * MAIN, CHIPS * TAIL))
    for chip in range(CHIPS):
        lanes = slice(TAIL * chip, TAIL * (chip + 1))
        store(chip, 4 * FL, jnp.concatenate([tails[k % 2][k // 2][:, lanes] for k in range(4)], axis=1))


def own_kernel(rows_ref, limit_ref, table_ref, twiddle_ref, out_ref):
    def store(chip, start, block):
        out_ref[chip, start : start + FL, :] = block

    transform(0, rows_ref, limit_ref, table_ref, twiddle_ref, store)


def other_kernel(own_ref, rows_ref, limit_ref, table_ref, twiddle_ref, out_ref):
    def store(chip, start, block):
        total = own_ref[chip, start : start + FL, :] + block
        out_ref[chip, start : start + FL, :] = total.astype(out_ref.dtype)

    transform(1, rows_ref, limit_ref, table_ref, twiddle_ref, store)


def add_kernel(got_ref, out_ref):
    def total(start, stop):
        sums = got_ref[0, start:stop, :].astype(jnp.float32)
        for chip in range(1, CHIPS):
            sums = sums + got_ref[chip, start:stop, :].astype(jnp.float32)
        return sums

    tail = total(4 * FL, 5 * FL)
    for part in range(2):
        for r in range(2):
            k = 2 * part + r
            main = total(k * FL, (k + 1) * FL)
            both = jnp.concatenate([main, tail[:, k * TAIL : (k + 1) * TAIL]], axis=1)
            out_ref[part, :, r, :] = both


def body(column_state, diffusivity, row_len, lat_rows, wave_order, tile_map):
    f32, bf16 = jnp.float32, jnp.bfloat16
    pos = (2 * lax.axis_index("x") + lax.axis_index("core")).astype(jnp.int32).reshape(1)
    smem = pl.BlockSpec(memory_space=pltpu.SMEM)
    vmem = pl.BlockSpec(memory_space=pltpu.VMEM)
    hbm = pl.BlockSpec(memory_space=pltpu.HBM)
    params = pltpu.CompilerParams(vmem_limit_bytes=VMEM)
    rows = pl.pallas_call(
        solve_kernel,
        out_shape=jax.ShapeDtypeStruct((ROWS, 2 * FL), bf16),
        in_specs=[hbm] * 3,
        out_specs=vmem,
        scratch_shapes=[
            pltpu.VMEM((LEV, NF, TILE_COLS), f32),
            pltpu.VMEM((LEV - 1, TILE_COLS), f32),
            pltpu.VMEM((1, TILE_COLS), jnp.int32),
            pltpu.VMEM((LEV, TILE_COLS), f32),
            pltpu.VMEM((LEV, NF, TILE_COLS), f32),
            pltpu.VMEM((FL, TILE_COLS), f32),
            pltpu.VMEM((2 * ROWS // 128, 8, 128), jnp.int32),
            pltpu.VMEM((ROWS, 2 * FL), f32),
            pltpu.SemaphoreType.DMA((6,)),
        ],
        compiler_params=pltpu.CompilerParams(vmem_limit_bytes=SOLVE_VMEM),
        name="solve",
    )(column_state, diffusivity, tile_map)
    table, twiddle, limit = pl.pallas_call(
        table_kernel,
        out_shape=[
            jax.ShapeDtypeStruct((2, BASE, 2 * SHARE), bf16),
            jax.ShapeDtypeStruct((4, 8, SHARE), f32),
            jax.ShapeDtypeStruct((4, 8, 2 * FL), jnp.int32),
        ],
        in_specs=[smem, smem, smem, vmem],
        out_specs=[vmem, vmem, vmem],
        compiler_params=params,
        cost_estimate=pl.CostEstimate(flops=40_000_000, bytes_accessed=2_200_000, transcendentals=0),
        name="tables",
    )(row_len, lat_rows, pos, wave_order.reshape(PEERS, OWN))
    rows = rows.reshape(SETS, CHUNK // 2, 2, 2 * FL)
    rows = lax.all_to_all(
        rows, "wide", split_axis=0, concat_axis=0, tiled=True, axis_index_groups=[list(ORDER)]
    )
    rows = rows.reshape(ROWS, 2 * FL)
    rows, table, twiddle, limit = lax.optimization_barrier((rows, table, twiddle, limit))
    got = lax.ppermute(rows, "core", [(0, 1), (1, 0)])
    own = pl.pallas_call(
        own_kernel,
        out_shape=jax.ShapeDtypeStruct((CHIPS, 5 * FL, MAIN), f32),
        in_specs=[vmem] * 4,
        out_specs=vmem,
        compiler_params=params,
        cost_estimate=pl.CostEstimate(flops=500_000_000, bytes_accessed=2_000_000, transcendentals=0),
        name="transform_own",
    )(rows, limit, table, twiddle)
    sums = pl.pallas_call(
        other_kernel,
        out_shape=jax.ShapeDtypeStruct((CHIPS, 5 * FL, MAIN), bf16),
        in_specs=[vmem] * 5,
        out_specs=vmem,
        compiler_params=params,
        name="transform_other",
    )(own, got, limit, table, twiddle)
    sums = lax.all_to_all(sums, "x", split_axis=0, concat_axis=0, tiled=True)
    return pl.pallas_call(
        add_kernel,
        out_shape=jax.ShapeDtypeStruct((2, FL, 2, OWN), f32),
        in_specs=[vmem],
        out_specs=vmem,
        compiler_params=params,
        name="add",
    )(sums)


def solution(mesh):
    chips = Mesh(mesh.devices.reshape(SETS, CHIPS, 2), ("wide", "x", "core"))
    columns = ("wide", "x", "core")
    return jax.shard_map(
        body,
        mesh=chips,
        in_specs=(
            P(None, None, columns),
            P(None, columns),
            P(),
            P("wide"),
            P(),
            P(columns, None),
        ),
        out_specs=P(None, None, "wide", ("x", "core")),
        check_vma=False,
    )
```

time: 59.9 us -> 58.3 us (0.973)
  Pallas kernels: 9.58 us -> 7.58 us
  starting transfers between devices: 25.1 us -> 25.9 us
  local copies, waits for them, and re-layouts: 2.08 us -> 1.43 us
    pallas_call x1, Pallas kernels: 3.53 us -> 2.33 us  [body(): pl.pallas_call(table_kernel, out_shape=[jax.ShapeDtypeStruct((2, BASE, 2...]
    pallas_call x1, Pallas kernels: 3.69 us -> 2.79 us  [body(): pl.pallas_call(solve_kernel, out_shape=jax.ShapeDtypeStruct((ROWS, 2 * FL...]
    ppermute x1, starting transfers between devices: 5.85 us -> 6.58 us  [body(): got = lax.ppermute(rows, 'core', [(0, 1), (1, 0)])]
    reshape x1, local copies, waits for them, and re-layouts: 0.77 us -> 0.07 us  [body(): wave_order.reshape(PEERS, OWN)]
    unnamed x4 -> x6, local copies, waits for them, and re-layouts: 1.31 us -> 1.36 us
  transfers between devices with their start and end apart: 2 -> 2, of which waited for: 2 -> 2; matrix products, arithmetic and copies ran while one was open for 1% -> 0% of each run, Pallas kernels for 7% -> 5%
where the time goes in v3:
time: 58.3 us; the launch traced here: 57.4 us
  starting transfers between devices  25.9 us (44%)
  waiting for transfers between devices  11.9 us (20%)
  blocking collectives  10.6 us (18%)
  Pallas kernels  7.58 us (13%)
  local copies, waits for them, and re-layouts  1.43 us (2%)
    all_to_all x1, starting transfers between devices, body(): lax.all_to_all(rows, 'wide', split_axis=0, concat_axis=0, tiled=True, axi...  19.3 us
    all_to_all x1, waiting for transfers between devices, body(): lax.all_to_all(rows, 'wide', split_axis=0, concat_axis=0, tiled=True, axi...  11.6 us
    all_to_all x1, blocking collectives, body(): sums = lax.all_to_all(sums, 'x', split_axis=0, concat_axis=0, tiled=True)  10.6 us
    ppermute x1, starting transfers between devices, body(): got = lax.ppermute(rows, 'core', [(0, 1), (1, 0)])  6.58 us
    pallas_call x1, Pallas kernels, body(): pl.pallas_call(solve_kernel, out_shape=jax.ShapeDtypeStruct((ROWS, 2 * FL...  2.79 us
    pallas_call x1, Pallas kernels, body(): pl.pallas_call(table_kernel, out_shape=[jax.ShapeDtypeStruct((2, BASE, 2...  2.33 us
    unnamed x6, local copies, waits for them, and re-layouts  1.36 us
  transfers between devices with their start and end apart: 2, of which 2 were waited for; matrix products, arithmetic and copies ran while one was open for 0% of the time, Pallas kernels for 5%

profile of v3, /device:TPU:1, one launch (start us, length us, event | category | flops | bytes accessed | tf_op | source)
XLA Modules:
  0.0 57.4 jit_solution(7909874779744628086)
XLA Ops:
  0.0 2.8 %solve.1 = bf16[768,128]{1,0:T(8,128)(2,1)} custom-call(f32[16,4,1408]{2,1,0:T(4,128)} %state_hbm.1, f32[15,1408]{1,0:T(8,128)} %diff_hbm.1, s32[1,1408]{1,0:T(1,128)} %map_hbm.1), custom_call_target="tpu_custom_call" | custom-call | tf_op jit(solution)/shard_map/solve/pallas_call | solution.py:245
  2.8 19.3 %all-to-all-start = ((bf16[64,6,2,128]{3,2,1,0:T(2,128)(2,1)}), bf16[64,6,2,128]{3,2,1,0:T(2,128)(2,1)S(1)}, u32[]{:S(2)}, u32[]{:S(2)}) async-start(bf16[64,6,2,128]{3,2,1,0:T(2,128)(2,1)} %bitcast.5), calls=%async_computation | async-start | bytes 393216 | tf_op jit(solution)/shard_map/all_to_all | solution.py:278
  22.1 0.0 copy-start.2
  22.1 0.7 %copy-done.2 = s32[1280]{0:T(1024)S(1)} copy-done((s32[1280]{0:T(1024)S(1)}, s32[1280]{0:T(1024)}, u32[]{:S(2)}) %copy-start.2) | copy-done | bytes 5144
  22.8 0.1 reshape.15.wave_ref
  22.9 0.0 copy-start
  22.9 0.0 copy-start.1
  22.9 0.7 %copy-done = s32[128]{0:T(128)S(1)} copy-done((s32[128]{0:T(128)S(1)}, s32[128]{0:T(128)}, u32[]{:S(2)}) %copy-start) | copy-done | bytes 536
  23.5 0.0 copy-done.1
  23.5 2.3 %tables.1 = (bf16[2,192,1280]{2,1,0:T(8,128)(2,1)S(1)}, f32[4,8,640]{2,1,0:T(8,128)S(1)}, s32[4,8,128]{2,1,0:T(8,128)S(1)}) custom-call(s32[128]{0:T(128)S(1)} %copy-done, s32[2]{0:T(128)S(1)} %copy-done.1, s32[1]{0:T(128)} %bitcast.2.pos_ref, s32[8,160]{1,0:T(8,128)S(1)} %reshape.15.wave_ref), custom_call_target="tpu_custom_call" | custom-call | flops 40000000 | bytes 2200000 | tf_op jit(solution)/shard_map/tables/pallas_call | solution.py:264
  25.9 11.6 %all-to-all-done = bf16[64,6,2,128]{3,2,1,0:T(2,128)(2,1)S(1)} async-done(((bf16[64,6,2,128]{3,2,1,0:T(2,128)(2,1)}), bf16[64,6,2,128]{3,2,1,0:T(2,128)(2,1)S(1)}, u32[]{:S(2)}, u32[]{:S(2)}) %all-to-all-start) | async-done | bytes 196640 | tf_op jit(solution)/shard_map/all_to_all | solution.py:278
  37.5 6.6 %collective-permute-start = (bf16[768,128]{1,0:T(8,128)(2,1)S(1)}, bf16[768,128]{1,0:T(8,128)(2,1)S(1)}, u32[]{:S(2)}, u32[]{:S(2)}) collective-permute-start(bf16[768,128]{1,0:T(8,128)(2,1)S(1)} %bitcast.3), channel_id=1, source_target_pairs={{0,1},{1,0},{2,3},{3,2},{4,5},{5,4},{6,7},{7,6},{8,9},{9,8},{10,11... | collective-permute-start | bytes 589832 | tf_op jit(solution)/shard_map/ppermute | solution.py:283
  44.1 0.8 %transform_own.1.own_ref = f32[4,320,128]{2,1,0:T(8,128)S(1)} custom-call(bf16[768,128]{1,0:T(8,128)(2,1)S(1)} %bitcast.4, s32[4,8,128]{2,1,0:T(8,128)S(1)} %get-tuple-element.16.limit_ref, bf16[2,192,1280]{2,1,0:T(8,128)(2,1)S(1)} %get-tuple-element.17.table_ref, f32[4,8,640]{2,1,0:T(8,128)S(1)} %get-tuple-element.18.twiddle_ref), custom_call_target="tpu_custom_call" | custom-call | flops 500000000 | bytes 2000000 | tf_op jit(solution)/shard_map/transform_own/pallas_call | solution.py:284
  44.9 0.2 collective-permute-done.rows_ref
  45.1 0.8 %transform_other.1 = bf16[4,320,128]{2,1,0:T(8,128)(2,1)S(1)} custom-call(f32[4,320,128]{2,1,0:T(8,128)S(1)} %transform_own.1.own_ref, bf16[768,128]{1,0:T(8,128)(2,1)S(1)} %collective-permute-done.rows_ref, s32[4,8,128]{2,1,0:T(8,128)S(1)} %get-tuple-element.16.limit_ref, bf16[2,192,1280]{2,1,0:T(8,128)(2,1)S(1)} %get-tuple-element.17.table_ref, ...), custom_call_target="tpu_custom_call" | custom-call | tf_op jit(solution)/shard_map/transform_other/pallas_call | solution.py:293
  46.0 10.6 %all_to_all.10.got_ref = bf16[4,320,128]{2,1,0:T(8,128)(2,1)S(1)} all-to-all(bf16[4,320,128]{2,1,0:T(8,128)(2,1)S(1)} %transform_other.1), channel_id=1, replica_groups=mesh['wide'=64,'x'=4,'core'=2] {'x'}, dimensions={0} | all-to-all | bytes 655360 | tf_op jit(solution)/shard_map/all_to_all | solution.py:301
  56.6 0.8 %add.5 = f32[2,64,2,160]{3,2,1,0:T(2,128)} custom-call(bf16[4,320,128]{2,1,0:T(8,128)(2,1)S(1)} %all_to_all.10.got_ref), custom_call_target="tpu_custom_call" | custom-call | tf_op jit(solution)/shard_map/add/pallas_call | solution.py:302
Async XLA Ops:
  2.8 34.7 %all-to-all-start = ((bf16[64,6,2,128]{3,2,1,0:T(2,128)(2,1)}), bf16[64,6,2,128]{3,2,1,0:T(2,128)(2,1)S(1)}, u32[]{:S(2)}, u32[]{:S(2)}) async-start(bf16[64,6,2,128]{3,2,1,0:T(2,128)(2,1)} %bitcast.5), calls=%async_computation | async-start | bytes 393216 | tf_op jit(solution)/shard_map/all_to_all | solution.py:278
  22.1 0.7 %copy-start.2 = (s32[1280]{0:T(1024)S(1)}, s32[1280]{0:T(1024)}, u32[]{:S(2)}) copy-start(s32[1280]{0:T(1024)} %param.10) | copy-start | bytes 15364
  22.9 0.7 %copy-start = (s32[128]{0:T(128)S(1)}, s32[128]{0:T(128)}, u32[]{:S(2)}) copy-start(s32[128]{0:T(128)} %len_ref.1) | copy-start | bytes 1540
  22.9 0.7 %copy-start.1 = (s32[2]{0:T(128)S(1)}, s32[2]{0:T(128)}, u32[]{:S(2)}) copy-start(s32[2]{0:T(128)} %lat_ref.1) | copy-start | bytes 28
  37.5 7.6 %collective-permute-start = (bf16[768,128]{1,0:T(8,128)(2,1)S(1)}, bf16[768,128]{1,0:T(8,128)(2,1)S(1)}, u32[]{:S(2)}, u32[]{:S(2)}) collective-permute-start(bf16[768,128]{1,0:T(8,128)(2,1)S(1)} %bitcast.3), channel_id=1, source_target_pairs={{0,1},{1,0},{2,3},{3,2},{4,5},{5,4},{6,7},{7,6},{8,9},{9,8},{10,11... | collective-permute-start | bytes 589832 | tf_op jit(solution)/shard_map/ppermute | solution.py:283

commit v4 on v3

--- a/solution.py
+++ b/solution.py
@@ -23,7 +23,7 @@
 PEERS = 8
 CHIPS = 4
 ROW_TILES = 4
-Z_ORDER = (0, 15, 1, 14, 2, 13, 3, 12, 4, 11, 5, 10, 6, 9, 7, 8)
+Z_ORDER = (8, 7, 9, 6, 10, 5, 11, 4, 12, 3, 13, 2, 14, 1, 15, 0)
 ORDER = tuple(z * ROW_TILES + y for z in Z_ORDER for y in range(ROW_TILES))
 SHARE = CHIPS * OWN
 VMEM = 40 * 1024 * 1024

time: 58.3 us -> 53.3 us (0.914)
  waiting for transfers between devices: 11.9 us -> 6.54 us
  starting transfers between devices: 25.9 us -> 26.7 us
    all_to_all x1, waiting for transfers between devices: 11.6 us -> 6.3 us  [body(): lax.all_to_all(rows, 'wide', split_axis=0, concat_axis=0, tiled=True, axi...]
    all_to_all x1, starting transfers between devices: 19.3 us -> 22.6 us  [body(): lax.all_to_all(rows, 'wide', split_axis=0, concat_axis=0, tiled=True, axi...]
    ppermute x1, starting transfers between devices: 6.58 us -> 4.14 us  [body(): got = lax.ppermute(rows, 'core', [(0, 1), (1, 0)])]
  transfers between devices with their start and end apart: 2 -> 2, of which waited for: 2 -> 2; matrix products, arithmetic and copies ran while one was open for 0% -> 0% of each run, Pallas kernels for 5% -> 6%
where the time goes in v4:
time: 53.3 us; the launch traced here: 53 us
  starting transfers between devices  26.7 us (50%)
  blocking collectives  10.6 us (20%)
  Pallas kernels  7.57 us (14%)
  waiting for transfers between devices  6.54 us (12%)
  local copies, waits for them, and re-layouts  1.43 us (3%)
    all_to_all x1, starting transfers between devices, body(): lax.all_to_all(rows, 'wide', split_axis=0, concat_axis=0, tiled=True, axi...  22.6 us
    all_to_all x1, blocking collectives, body(): sums = lax.all_to_all(sums, 'x', split_axis=0, concat_axis=0, tiled=True)  10.6 us
    all_to_all x1, waiting for transfers between devices, body(): lax.all_to_all(rows, 'wide', split_axis=0, concat_axis=0, tiled=True, axi...  6.3 us
    ppermute x1, starting transfers between devices, body(): got = lax.ppermute(rows, 'core', [(0, 1), (1, 0)])  4.14 us
    pallas_call x1, Pallas kernels, body(): pl.pallas_call(solve_kernel, out_shape=jax.ShapeDtypeStruct((ROWS, 2 * FL...  2.79 us
    pallas_call x1, Pallas kernels, body(): pl.pallas_call(table_kernel, out_shape=[jax.ShapeDtypeStruct((2, BASE, 2...  2.33 us
    unnamed x6, local copies, waits for them, and re-layouts  1.36 us
  transfers between devices with their start and end apart: 2, of which 2 were waited for; matrix products, arithmetic and copies ran while one was open for 0% of the time, Pallas kernels for 6%

profile of v4, /device:TPU:1, one launch (start us, length us, event | category | flops | bytes accessed | tf_op | source)
XLA Modules:
  0.0 53.0 jit_solution(14332090646667084782)
XLA Ops:
  0.0 2.8 %solve.1 = bf16[768,128]{1,0:T(8,128)(2,1)} custom-call(f32[16,4,1408]{2,1,0:T(4,128)} %state_hbm.1, f32[15,1408]{1,0:T(8,128)} %diff_hbm.1, s32[1,1408]{1,0:T(1,128)} %map_hbm.1), custom_call_target="tpu_custom_call" | custom-call | tf_op jit(solution)/shard_map/solve/pallas_call | solution.py:245
  2.8 22.6 %all-to-all-start = ((bf16[64,6,2,128]{3,2,1,0:T(2,128)(2,1)}), bf16[64,6,2,128]{3,2,1,0:T(2,128)(2,1)S(1)}, u32[]{:S(2)}, u32[]{:S(2)}) async-start(bf16[64,6,2,128]{3,2,1,0:T(2,128)(2,1)} %bitcast.5), calls=%async_computation | async-start | bytes 393216 | tf_op jit(solution)/shard_map/all_to_all | solution.py:278
  25.4 0.0 copy-start.2
  25.4 0.7 %copy-done.2 = s32[1280]{0:T(1024)S(1)} copy-done((s32[1280]{0:T(1024)S(1)}, s32[1280]{0:T(1024)}, u32[]{:S(2)}) %copy-start.2) | copy-done | bytes 5144
  26.1 0.1 reshape.15.wave_ref
  26.2 0.0 copy-start
  26.2 0.0 copy-start.1
  26.2 0.7 %copy-done = s32[128]{0:T(128)S(1)} copy-done((s32[128]{0:T(128)S(1)}, s32[128]{0:T(128)}, u32[]{:S(2)}) %copy-start) | copy-done | bytes 536
  26.8 0.0 copy-done.1
  26.8 2.3 %tables.1 = (bf16[2,192,1280]{2,1,0:T(8,128)(2,1)S(1)}, f32[4,8,640]{2,1,0:T(8,128)S(1)}, s32[4,8,128]{2,1,0:T(8,128)S(1)}) custom-call(s32[128]{0:T(128)S(1)} %copy-done, s32[2]{0:T(128)S(1)} %copy-done.1, s32[1]{0:T(128)} %bitcast.2.pos_ref, s32[8,160]{1,0:T(8,128)S(1)} %reshape.15.wave_ref), custom_call_target="tpu_custom_call" | custom-call | flops 40000000 | bytes 2200000 | tf_op jit(solution)/shard_map/tables/pallas_call | solution.py:264
  29.2 6.3 %all-to-all-done = bf16[64,6,2,128]{3,2,1,0:T(2,128)(2,1)S(1)} async-done(((bf16[64,6,2,128]{3,2,1,0:T(2,128)(2,1)}), bf16[64,6,2,128]{3,2,1,0:T(2,128)(2,1)S(1)}, u32[]{:S(2)}, u32[]{:S(2)}) %all-to-all-start) | async-done | bytes 196640 | tf_op jit(solution)/shard_map/all_to_all | solution.py:278
  35.5 4.1 %collective-permute-start = (bf16[768,128]{1,0:T(8,128)(2,1)S(1)}, bf16[768,128]{1,0:T(8,128)(2,1)S(1)}, u32[]{:S(2)}, u32[]{:S(2)}) collective-permute-start(bf16[768,128]{1,0:T(8,128)(2,1)S(1)} %bitcast.3), channel_id=1, source_target_pairs={{0,1},{1,0},{2,3},{3,2},{4,5},{5,4},{6,7},{7,6},{8,9},{9,8},{10,11... | collective-permute-start | bytes 589832 | tf_op jit(solution)/shard_map/ppermute | solution.py:283
  39.6 0.8 %transform_own.1.own_ref = f32[4,320,128]{2,1,0:T(8,128)S(1)} custom-call(bf16[768,128]{1,0:T(8,128)(2,1)S(1)} %bitcast.4, s32[4,8,128]{2,1,0:T(8,128)S(1)} %get-tuple-element.16.limit_ref, bf16[2,192,1280]{2,1,0:T(8,128)(2,1)S(1)} %get-tuple-element.17.table_ref, f32[4,8,640]{2,1,0:T(8,128)S(1)} %get-tuple-element.18.twiddle_ref), custom_call_target="tpu_custom_call" | custom-call | flops 500000000 | bytes 2000000 | tf_op jit(solution)/shard_map/transform_own/pallas_call | solution.py:284
  40.4 0.2 collective-permute-done.rows_ref
  40.7 0.8 %transform_other.1 = bf16[4,320,128]{2,1,0:T(8,128)(2,1)S(1)} custom-call(f32[4,320,128]{2,1,0:T(8,128)S(1)} %transform_own.1.own_ref, bf16[768,128]{1,0:T(8,128)(2,1)S(1)} %collective-permute-done.rows_ref, s32[4,8,128]{2,1,0:T(8,128)S(1)} %get-tuple-element.16.limit_ref, bf16[2,192,1280]{2,1,0:T(8,128)(2,1)S(1)} %get-tuple-element.17.table_ref, ...), custom_call_target="tpu_custom_call" | custom-call | tf_op jit(solution)/shard_map/transform_other/pallas_call | solution.py:293
  41.5 10.6 %all_to_all.10.got_ref = bf16[4,320,128]{2,1,0:T(8,128)(2,1)S(1)} all-to-all(bf16[4,320,128]{2,1,0:T(8,128)(2,1)S(1)} %transform_other.1), channel_id=1, replica_groups=mesh['wide'=64,'x'=4,'core'=2] {'x'}, dimensions={0} | all-to-all | bytes 655360 | tf_op jit(solution)/shard_map/all_to_all | solution.py:301
  52.1 0.8 %add.5 = f32[2,64,2,160]{3,2,1,0:T(2,128)} custom-call(bf16[4,320,128]{2,1,0:T(8,128)(2,1)S(1)} %all_to_all.10.got_ref), custom_call_target="tpu_custom_call" | custom-call | tf_op jit(solution)/shard_map/add/pallas_call | solution.py:302
Async XLA Ops:
  2.8 32.7 %all-to-all-start = ((bf16[64,6,2,128]{3,2,1,0:T(2,128)(2,1)}), bf16[64,6,2,128]{3,2,1,0:T(2,128)(2,1)S(1)}, u32[]{:S(2)}, u32[]{:S(2)}) async-start(bf16[64,6,2,128]{3,2,1,0:T(2,128)(2,1)} %bitcast.5), calls=%async_computation | async-start | bytes 393216 | tf_op jit(solution)/shard_map/all_to_all | solution.py:278
  25.4 0.7 %copy-start.2 = (s32[1280]{0:T(1024)S(1)}, s32[1280]{0:T(1024)}, u32[]{:S(2)}) copy-start(s32[1280]{0:T(1024)} %param.10) | copy-start | bytes 15364
  26.2 0.7 %copy-start = (s32[128]{0:T(128)S(1)}, s32[128]{0:T(128)}, u32[]{:S(2)}) copy-start(s32[128]{0:T(128)} %len_ref.1) | copy-start | bytes 1540
  26.2 0.7 %copy-start.1 = (s32[2]{0:T(128)S(1)}, s32[2]{0:T(128)}, u32[]{:S(2)}) copy-start(s32[2]{0:T(128)} %lat_ref.1) | copy-start | bytes 28
  35.5 5.2 %collective-permute-start = (bf16[768,128]{1,0:T(8,128)(2,1)S(1)}, bf16[768,128]{1,0:T(8,128)(2,1)S(1)}, u32[]{:S(2)}, u32[]{:S(2)}) collective-permute-start(bf16[768,128]{1,0:T(8,128)(2,1)S(1)} %bitcast.3), channel_id=1, source_target_pairs={{0,1},{1,0},{2,3},{3,2},{4,5},{5,4},{6,7},{7,6},{8,9},{9,8},{10,11... | collective-permute-start | bytes 589832 | tf_op jit(solution)/shard_map/ppermute | solution.py:283

commit v5 on v4

--- a/solution.py
+++ b/solution.py
@@ -22,9 +22,11 @@
 TAIL = OWN - MAIN
 PEERS = 8
 CHIPS = 4
+X_ORDER = (2, 1, 3, 0)
 ROW_TILES = 4
-Z_ORDER = (8, 7, 9, 6, 10, 5, 11, 4, 12, 3, 13, 2, 14, 1, 15, 0)
-ORDER = tuple(z * ROW_TILES + y for z in Z_ORDER for y in range(ROW_TILES))
+Z_ORDER = (10, 9, 11, 8, 12, 7, 13, 6, 14, 5, 15, 4, 0, 3, 1, 2)
+Y_FIRST = 2
+ORDER = tuple(z * ROW_TILES + (Y_FIRST + y) % ROW_TILES for z in Z_ORDER for y in range(ROW_TILES))
 SHARE = CHIPS * OWN
 VMEM = 40 * 1024 * 1024
 SOLVE_VMEM = 62 * 1024 * 1024
@@ -32,6 +34,12 @@
 
 def lane_gather(values, lanes):
     return jnp.take_along_axis(values, lanes, axis=1, mode="promise_in_bounds")
+
+
+def tile_of(listed):
+    z = jnp.floor((listed + 0.5) * (1.0 / ROW_TILES))
+    y = listed - ROW_TILES * z + Y_FIRST
+    return ROW_TILES * z + jnp.where(y >= ROW_TILES, y - ROW_TILES, y)
 
 
 def solve_kernel(state_hbm, diff_hbm, map_hbm, out_ref, state_ref, diff_ref, map_ref, ratio_ref, value_ref, cols_ref, pick_ref, rows_ref, sems):
@@ -48,9 +56,11 @@
             place = (lax.broadcasted_iota(jnp.int32, (8, 128), 1) + 128 * tile).astype(jnp.float32)
             chunk = jnp.floor((place + 0.5) * (1.0 / CHUNK))
             inner = place - CHUNK * chunk
-            slot = (PIECE * chunk + 2.0 * inner + part).astype(jnp.int32)
-            lo_tile = (PIECE * (128 * tile // CHUNK)) // 128
-            hi_tile = min(TILE_COLS // 128 - 1, (PIECE * ((128 * tile + 127) // CHUNK) + PIECE - 1) // 128)
+            slot = (PIECE * tile_of(chunk) + 2.0 * inner + part).astype(jnp.int32)
+            span = PIECE * ROW_TILES
+            step = CHUNK * ROW_TILES
+            lo_tile = (span * (128 * tile // step)) // 128
+            hi_tile = min(TILE_COLS // 128 - 1, (span * ((128 * tile + 127) // step + 1) - 1) // 128)
             column = jnp.full((8, 128), -1, jnp.int32)
             for k in range(lo_tile, hi_tile + 1):
                 entries = jnp.broadcast_to(map_ref[0:1, 128 * k : 128 * (k + 1)], (8, 128))
@@ -142,7 +152,7 @@
                 row = lax.broadcasted_iota(jnp.int32, (rows, SHARE), 0) + (first + part * rows)
                 row = row.astype(jnp.float32)
                 group = jnp.floor((row + 0.5) * (1.0 / CHUNK))
-                slot = 8.0 * PIECE * group + 2.0 * (row - CHUNK * group)
+                slot = 8.0 * PIECE * tile_of(group) + 2.0 * (row - CHUNK * group)
                 cosine, sine = cos_sin_turns(turns_of(slot * waves, length, inverse))
                 cosines.append(cosine)
                 sines.append(-sine)
@@ -182,7 +192,8 @@
     lane = lax.broadcasted_iota(jnp.int32, (HALF, 2 * FL), 1)
     group = row // CHUNK
     inner = row - CHUNK * group
-    slot = 8 * PIECE * group + 2 * inner + jnp.where(lane >= FL, 1, 0)
+    tile = group // ROW_TILES * ROW_TILES + (group + Y_FIRST) % ROW_TILES
+    slot = 8 * PIECE * tile + 2 * inner + jnp.where(lane >= FL, 1, 0)
     slot = jnp.where(inner == CHUNK - 1, 1 << 20, slot)
     step = ROW_TILES * CHUNK
     tails = []
@@ -214,7 +225,7 @@
 def other_kernel(own_ref, rows_ref, limit_ref, table_ref, twiddle_ref, out_ref):
     def store(chip, start, block):
         total = own_ref[chip, start : start + FL, :] + block
-        out_ref[chip, start : start + FL, :] = total.astype(out_ref.dtype)
+        out_ref[X_ORDER.index(chip), start : start + FL, :] = total.astype(out_ref.dtype)
 
     transform(1, rows_ref, limit_ref, table_ref, twiddle_ref, store)
 
@@ -298,7 +309,9 @@
         compiler_params=params,
         name="transform_other",
     )(own, got, limit, table, twiddle)
-    sums = lax.all_to_all(sums, "x", split_axis=0, concat_axis=0, tiled=True)
+    sums = lax.all_to_all(
+        sums, "x", split_axis=0, concat_axis=0, tiled=True, axis_index_groups=[list(X_ORDER)]
+    )
     return pl.pallas_call(
         add_kernel,
         out_shape=jax.ShapeDtypeStruct((2, FL, 2, OWN), f32),

time: 53.3 us -> 50.5 us (0.947)
  starting transfers between devices: 26.7 us -> 25.3 us
  blocking collectives: 10.6 us -> 9.59 us
  waiting for transfers between devices: 6.54 us -> 5.6 us
  Pallas kernels: 7.57 us -> 8.15 us
    all_to_all x1, starting transfers between devices: 22.6 us -> 21.4 us  [body(): lax.all_to_all(rows, 'wide', split_axis=0, concat_axis=0, tiled=True, axi...]
    all_to_all x1, blocking collectives: 10.6 us -> 9.59 us  [body(): lax.all_to_all(sums, 'x', split_axis=0, concat_axis=0, tiled=True, axis_i...]
    all_to_all x1, waiting for transfers between devices: 6.3 us -> 5.57 us  [body(): lax.all_to_all(rows, 'wide', split_axis=0, concat_axis=0, tiled=True, axi...]
  transfers between devices with their start and end apart: 2 -> 2, of which waited for: 2 -> 1; matrix products, arithmetic and copies ran while one was open for 0% -> 0% of each run, Pallas kernels for 6% -> 7%
where the time goes in v5:
time: 50.5 us; the launch traced here: 50.2 us
  starting transfers between devices  25.3 us (50%)
  blocking collectives  9.59 us (19%)
  Pallas kernels  8.15 us (16%)
  waiting for transfers between devices  5.6 us (11%)
  local copies, waits for them, and re-layouts  1.43 us (3%)
    all_to_all x1, starting transfers between devices, body(): lax.all_to_all(rows, 'wide', split_axis=0, concat_axis=0, tiled=True, axi...  21.4 us
    all_to_all x1, blocking collectives, body(): lax.all_to_all(sums, 'x', split_axis=0, concat_axis=0, tiled=True, axis_i...  9.59 us
    all_to_all x1, waiting for transfers between devices, body(): lax.all_to_all(rows, 'wide', split_axis=0, concat_axis=0, tiled=True, axi...  5.57 us
    ppermute x1, starting transfers between devices, body(): got = lax.ppermute(rows, 'core', [(0, 1), (1, 0)])  3.89 us
    pallas_call x1, Pallas kernels, body(): pl.pallas_call(solve_kernel, out_shape=jax.ShapeDtypeStruct((ROWS, 2 * FL...  2.79 us
    pallas_call x1, Pallas kernels, body(): pl.pallas_call(table_kernel, out_shape=[jax.ShapeDtypeStruct((2, BASE, 2...  2.5 us
    unnamed x6, local copies, waits for them, and re-layouts  1.36 us
    pallas_call x1, Pallas kernels, body(): pl.pallas_call(other_kernel, out_shape=jax.ShapeDtypeStruct((CHIPS, 5 * F...  1.01 us
  transfers between devices with their start and end apart: 2, of which 1 were waited for; matrix products, arithmetic and copies ran while one was open for 0% of the time, Pallas kernels for 7%

profile of v5, /device:TPU:1, one launch (start us, length us, event | category | flops | bytes accessed | tf_op | source)
XLA Modules:
  0.0 50.2 jit_solution(773625336717384440)
XLA Ops:
  0.0 2.8 %solve.1 = bf16[768,128]{1,0:T(8,128)(2,1)} custom-call(f32[16,4,1408]{2,1,0:T(4,128)} %state_hbm.1, f32[15,1408]{1,0:T(8,128)} %diff_hbm.1, s32[1,1408]{1,0:T(1,128)} %map_hbm.1), custom_call_target="tpu_custom_call" | custom-call | tf_op jit(solution)/shard_map/solve/pallas_call | solution.py:256
  2.8 21.4 %all-to-all-start = ((bf16[64,6,2,128]{3,2,1,0:T(2,128)(2,1)}), bf16[64,6,2,128]{3,2,1,0:T(2,128)(2,1)S(1)}, u32[]{:S(2)}, u32[]{:S(2)}) async-start(bf16[64,6,2,128]{3,2,1,0:T(2,128)(2,1)} %bitcast.5), calls=%async_computation | async-start | bytes 393216 | tf_op jit(solution)/shard_map/all_to_all | solution.py:289
  24.3 0.0 copy-start.2
  24.3 0.7 %copy-done.2 = s32[1280]{0:T(1024)S(1)} copy-done((s32[1280]{0:T(1024)S(1)}, s32[1280]{0:T(1024)}, u32[]{:S(2)}) %copy-start.2) | copy-done | bytes 5144
  25.0 0.1 reshape.15.wave_ref
  25.0 0.0 copy-start
  25.0 0.0 copy-start.1
  25.0 0.7 %copy-done = s32[128]{0:T(128)S(1)} copy-done((s32[128]{0:T(128)S(1)}, s32[128]{0:T(128)}, u32[]{:S(2)}) %copy-start) | copy-done | bytes 536
  25.7 0.0 copy-done.1
  25.7 2.5 %tables.1 = (bf16[2,192,1280]{2,1,0:T(8,128)(2,1)S(1)}, f32[4,8,640]{2,1,0:T(8,128)S(1)}, s32[4,8,128]{2,1,0:T(8,128)S(1)}) custom-call(s32[128]{0:T(128)S(1)} %copy-done, s32[2]{0:T(128)S(1)} %copy-done.1, s32[1]{0:T(128)} %bitcast.2.pos_ref, s32[8,160]{1,0:T(8,128)S(1)} %reshape.15.wave_ref), custom_call_target="tpu_custom_call" | custom-call | flops 40000000 | bytes 2200000 | tf_op jit(solution)/shard_map/tables/pallas_call | solution.py:275
  28.2 5.6 %all-to-all-done = bf16[64,6,2,128]{3,2,1,0:T(2,128)(2,1)S(1)} async-done(((bf16[64,6,2,128]{3,2,1,0:T(2,128)(2,1)}), bf16[64,6,2,128]{3,2,1,0:T(2,128)(2,1)S(1)}, u32[]{:S(2)}, u32[]{:S(2)}) %all-to-all-start) | async-done | bytes 196640 | tf_op jit(solution)/shard_map/all_to_all | solution.py:289
  33.8 3.9 %collective-permute-start = (bf16[768,128]{1,0:T(8,128)(2,1)S(1)}, bf16[768,128]{1,0:T(8,128)(2,1)S(1)}, u32[]{:S(2)}, u32[]{:S(2)}) collective-permute-start(bf16[768,128]{1,0:T(8,128)(2,1)S(1)} %bitcast.3), channel_id=1, source_target_pairs={{0,1},{1,0},{2,3},{3,2},{4,5},{5,4},{6,7},{7,6},{8,9},{9,8},{10,11... | collective-permute-start | bytes 589832 | tf_op jit(solution)/shard_map/ppermute | solution.py:294
  37.7 1.0 %transform_own.1.own_ref = f32[4,320,128]{2,1,0:T(8,128)S(1)} custom-call(bf16[768,128]{1,0:T(8,128)(2,1)S(1)} %bitcast.4, s32[4,8,128]{2,1,0:T(8,128)S(1)} %get-tuple-element.16.limit_ref, bf16[2,192,1280]{2,1,0:T(8,128)(2,1)S(1)} %get-tuple-element.17.table_ref, f32[4,8,640]{2,1,0:T(8,128)S(1)} %get-tuple-element.18.twiddle_ref), custom_call_target="tpu_custom_call" | custom-call | flops 500000000 | bytes 2000000 | tf_op jit(solution)/shard_map/transform_own/pallas_call | solution.py:295
  38.7 0.0 collective-permute-done.rows_ref
  38.7 1.0 %transform_other.1 = bf16[4,320,128]{2,1,0:T(8,128)(2,1)S(1)} custom-call(f32[4,320,128]{2,1,0:T(8,128)S(1)} %transform_own.1.own_ref, bf16[768,128]{1,0:T(8,128)(2,1)S(1)} %collective-permute-done.rows_ref, s32[4,8,128]{2,1,0:T(8,128)S(1)} %get-tuple-element.16.limit_ref, bf16[2,192,1280]{2,1,0:T(8,128)(2,1)S(1)} %get-tuple-element.17.table_ref, ...), custom_call_target="tpu_custom_call" | custom-call | tf_op jit(solution)/shard_map/transform_other/pallas_call | solution.py:304
  39.7 9.6 %all_to_all.10.got_ref = bf16[4,320,128]{2,1,0:T(8,128)(2,1)S(1)} all-to-all(bf16[4,320,128]{2,1,0:T(8,128)(2,1)S(1)} %transform_other.1), channel_id=1, replica_groups={{4,2,6,0},{5,3,7,1},{12,10,14,8},{13,11,15,9},{20,18,22,16},{21,19,23,1..., dimensions={0} | all-to-all | bytes 655360 | tf_op jit(solution)/shard_map/all_to_all | solution.py:312
  49.3 0.8 %add.5 = f32[2,64,2,160]{3,2,1,0:T(2,128)} custom-call(bf16[4,320,128]{2,1,0:T(8,128)(2,1)S(1)} %all_to_all.10.got_ref), custom_call_target="tpu_custom_call" | custom-call | tf_op jit(solution)/shard_map/add/pallas_call | solution.py:315
Async XLA Ops:
  2.8 31.0 %all-to-all-start = ((bf16[64,6,2,128]{3,2,1,0:T(2,128)(2,1)}), bf16[64,6,2,128]{3,2,1,0:T(2,128)(2,1)S(1)}, u32[]{:S(2)}, u32[]{:S(2)}) async-start(bf16[64,6,2,128]{3,2,1,0:T(2,128)(2,1)} %bitcast.5), calls=%async_computation | async-start | bytes 393216 | tf_op jit(solution)/shard_map/all_to_all | solution.py:289
  24.3 0.7 %copy-start.2 = (s32[1280]{0:T(1024)S(1)}, s32[1280]{0:T(1024)}, u32[]{:S(2)}) copy-start(s32[1280]{0:T(1024)} %param.10) | copy-start | bytes 15364
  25.0 0.7 %copy-start = (s32[128]{0:T(128)S(1)}, s32[128]{0:T(128)}, u32[]{:S(2)}) copy-start(s32[128]{0:T(128)} %len_ref.1) | copy-start | bytes 1540
  25.0 0.7 %copy-start.1 = (s32[2]{0:T(128)S(1)}, s32[2]{0:T(128)}, u32[]{:S(2)}) copy-start(s32[2]{0:T(128)} %lat_ref.1) | copy-start | bytes 28
  33.8 4.9 %collective-permute-start = (bf16[768,128]{1,0:T(8,128)(2,1)S(1)}, bf16[768,128]{1,0:T(8,128)(2,1)S(1)}, u32[]{:S(2)}, u32[]{:S(2)}) collective-permute-start(bf16[768,128]{1,0:T(8,128)(2,1)S(1)} %bitcast.3), channel_id=1, source_target_pairs={{0,1},{1,0},{2,3},{3,2},{4,5},{5,4},{6,7},{7,6},{8,9},{9,8},{10,11... | collective-permute-start | bytes 589832 | tf_op jit(solution)/shard_map/ppermute | solution.py:294

commit v6 on v5

--- a/solution.py
+++ b/solution.py
@@ -42,7 +42,7 @@
     return ROW_TILES * z + jnp.where(y >= ROW_TILES, y - ROW_TILES, y)
 
 
-def solve_kernel(state_hbm, diff_hbm, map_hbm, out_ref, state_ref, diff_ref, map_ref, ratio_ref, value_ref, cols_ref, pick_ref, rows_ref, sems):
+def solve_kernel(state_hbm, diff_hbm, map_hbm, out_ref, state_ref, diff_ref, map_ref, ratio_ref, value_ref, cols_ref, pick_ref, rows_ref, sent_ref, sems, out_sems):
     copies = [pltpu.make_async_copy(map_hbm, map_ref, sems.at[0]), pltpu.make_async_copy(diff_hbm, diff_ref, sems.at[1])]
     for part in range(4):
         levels = pl.ds(4 * part, 4)
@@ -89,6 +89,7 @@
     for lev in range(LEV - 2, -1, -1):
         solved = value_ref[lev] - ratio_ref[lev : lev + 1, :] * solved
         cols_ref[lev * NF : (lev + 1) * NF, :] = solved
+    sent = []
     for tile in range(tiles):
         blocks = []
         for part in range(2):
@@ -103,10 +104,15 @@
                     block = jnp.where(hits[k], found, block)
                 blocks.append(block)
         rows_ref[128 * tile : 128 * (tile + 1), :] = jnp.concatenate(blocks, axis=0).T
-    step = ROW_TILES * CHUNK
-    for place, z in enumerate(Z_ORDER):
-        block = rows_ref[step * z : step * (z + 1), :]
-        out_ref[step * place : step * (place + 1), :] = block.astype(jnp.bfloat16)
+        step = ROW_TILES * CHUNK
+        for z in range(128 * tile // step, 128 * (tile + 1) // step):
+            place = pl.ds(step * Z_ORDER.index(z), step)
+            sent_ref[place, :] = rows_ref[step * z : step * (z + 1), :].astype(jnp.bfloat16)
+            copy = pltpu.make_async_copy(sent_ref.at[place], out_ref.at[place], out_sems.at[z])
+            copy.start()
+            sent.append(copy)
+    for copy in sent:
+        copy.wait()
 
 
 def cos_sin_turns(turns):
@@ -257,7 +263,7 @@
         solve_kernel,
         out_shape=jax.ShapeDtypeStruct((ROWS, 2 * FL), bf16),
         in_specs=[hbm] * 3,
-        out_specs=vmem,
+        out_specs=hbm,
         scratch_shapes=[
             pltpu.VMEM((LEV, NF, TILE_COLS), f32),
             pltpu.VMEM((LEV - 1, TILE_COLS), f32),
@@ -267,7 +273,9 @@
             pltpu.VMEM((FL, TILE_COLS), f32),
             pltpu.VMEM((2 * ROWS // 128, 8, 128), jnp.int32),
             pltpu.VMEM((ROWS, 2 * FL), f32),
+            pltpu.VMEM((ROWS, 2 * FL), bf16),
             pltpu.SemaphoreType.DMA((6,)),
+            pltpu.SemaphoreType.DMA((len(Z_ORDER),)),
         ],
         compiler_params=pltpu.CompilerParams(vmem_limit_bytes=SOLVE_VMEM),
         name="solve",

time: 50.5 us -> 50.6 us (level)
  no operation moved by 1% of the time
where the time goes in v6:
time: 50.6 us; the launch traced here: 50.2 us
  starting transfers between devices  25.3 us (50%)
  blocking collectives  9.6 us (19%)
  Pallas kernels  8.21 us (16%)
  waiting for transfers between devices  5.61 us (11%)
  local copies, waits for them, and re-layouts  1.43 us (3%)
    all_to_all x1, starting transfers between devices, body(): lax.all_to_all(rows, 'wide', split_axis=0, concat_axis=0, tiled=True, axi...  21.4 us
    all_to_all x1, blocking collectives, body(): lax.all_to_all(sums, 'x', split_axis=0, concat_axis=0, tiled=True, axis_i...  9.6 us
    all_to_all x1, waiting for transfers between devices, body(): lax.all_to_all(rows, 'wide', split_axis=0, concat_axis=0, tiled=True, axi...  5.57 us
    ppermute x1, starting transfers between devices, body(): got = lax.ppermute(rows, 'core', [(0, 1), (1, 0)])  3.89 us
    pallas_call x1, Pallas kernels, body(): pl.pallas_call(solve_kernel, out_shape=jax.ShapeDtypeStruct((ROWS, 2 * FL...  2.85 us
    pallas_call x1, Pallas kernels, body(): pl.pallas_call(table_kernel, out_shape=[jax.ShapeDtypeStruct((2, BASE, 2...  2.5 us
    unnamed x6, local copies, waits for them, and re-layouts  1.36 us
  transfers between devices with their start and end apart: 2, of which 1 were waited for; matrix products, arithmetic and copies ran while one was open for 0% of the time, Pallas kernels for 7%

profile of v6, /device:TPU:1, one launch (start us, length us, event | category | flops | bytes accessed | tf_op | source)
XLA Modules:
  0.0 50.2 jit_solution(3221932573964914249)
XLA Ops:
  0.0 2.9 %solve.1 = bf16[768,128]{1,0:T(8,128)(2,1)} custom-call(f32[16,4,1408]{2,1,0:T(4,128)} %state_hbm.1, f32[15,1408]{1,0:T(8,128)} %diff_hbm.1, s32[1,1408]{1,0:T(1,128)} %map_hbm.1), custom_call_target="tpu_custom_call" | custom-call | tf_op jit(solution)/shard_map/solve/pallas_call | solution.py:262
  2.9 21.4 %all-to-all-start = ((bf16[64,6,2,128]{3,2,1,0:T(2,128)(2,1)}), bf16[64,6,2,128]{3,2,1,0:T(2,128)(2,1)S(1)}, u32[]{:S(2)}, u32[]{:S(2)}) async-start(bf16[64,6,2,128]{3,2,1,0:T(2,128)(2,1)} %bitcast.5), calls=%async_computation | async-start | bytes 393216 | tf_op jit(solution)/shard_map/all_to_all | solution.py:297
  24.3 0.0 copy-start.2
  24.3 0.7 %copy-done.2 = s32[1280]{0:T(1024)S(1)} copy-done((s32[1280]{0:T(1024)S(1)}, s32[1280]{0:T(1024)}, u32[]{:S(2)}) %copy-start.2) | copy-done | bytes 5144
  25.0 0.1 reshape.15.wave_ref
  25.1 0.0 copy-start
  25.1 0.0 copy-start.1
  25.1 0.7 %copy-done = s32[128]{0:T(128)S(1)} copy-done((s32[128]{0:T(128)S(1)}, s32[128]{0:T(128)}, u32[]{:S(2)}) %copy-start) | copy-done | bytes 536
  25.7 0.0 copy-done.1
  25.8 2.5 %tables.1 = (bf16[2,192,1280]{2,1,0:T(8,128)(2,1)S(1)}, f32[4,8,640]{2,1,0:T(8,128)S(1)}, s32[4,8,128]{2,1,0:T(8,128)S(1)}) custom-call(s32[128]{0:T(128)S(1)} %copy-done, s32[2]{0:T(128)S(1)} %copy-done.1, s32[1]{0:T(128)} %bitcast.2.pos_ref, s32[8,160]{1,0:T(8,128)S(1)} %reshape.15.wave_ref), custom_call_target="tpu_custom_call" | custom-call | flops 40000000 | bytes 2200000 | tf_op jit(solution)/shard_map/tables/pallas_call | solution.py:283
  28.3 5.6 %all-to-all-done = bf16[64,6,2,128]{3,2,1,0:T(2,128)(2,1)S(1)} async-done(((bf16[64,6,2,128]{3,2,1,0:T(2,128)(2,1)}), bf16[64,6,2,128]{3,2,1,0:T(2,128)(2,1)S(1)}, u32[]{:S(2)}, u32[]{:S(2)}) %all-to-all-start) | async-done | bytes 196640 | tf_op jit(solution)/shard_map/all_to_all | solution.py:297
  33.8 3.9 %collective-permute-start = (bf16[768,128]{1,0:T(8,128)(2,1)S(1)}, bf16[768,128]{1,0:T(8,128)(2,1)S(1)}, u32[]{:S(2)}, u32[]{:S(2)}) collective-permute-start(bf16[768,128]{1,0:T(8,128)(2,1)S(1)} %bitcast.3), channel_id=1, source_target_pairs={{0,1},{1,0},{2,3},{3,2},{4,5},{5,4},{6,7},{7,6},{8,9},{9,8},{10,11... | collective-permute-start | bytes 589832 | tf_op jit(solution)/shard_map/ppermute | solution.py:302
  37.7 1.0 %transform_own.1.own_ref = f32[4,320,128]{2,1,0:T(8,128)S(1)} custom-call(bf16[768,128]{1,0:T(8,128)(2,1)S(1)} %bitcast.4, s32[4,8,128]{2,1,0:T(8,128)S(1)} %get-tuple-element.16.limit_ref, bf16[2,192,1280]{2,1,0:T(8,128)(2,1)S(1)} %get-tuple-element.17.table_ref, f32[4,8,640]{2,1,0:T(8,128)S(1)} %get-tuple-element.18.twiddle_ref), custom_call_target="tpu_custom_call" | custom-call | flops 500000000 | bytes 2000000 | tf_op jit(solution)/shard_map/transform_own/pallas_call | solution.py:303
  38.7 0.0 collective-permute-done.rows_ref
  38.8 1.0 %transform_other.1 = bf16[4,320,128]{2,1,0:T(8,128)(2,1)S(1)} custom-call(f32[4,320,128]{2,1,0:T(8,128)S(1)} %transform_own.1.own_ref, bf16[768,128]{1,0:T(8,128)(2,1)S(1)} %collective-permute-done.rows_ref, s32[4,8,128]{2,1,0:T(8,128)S(1)} %get-tuple-element.16.limit_ref, bf16[2,192,1280]{2,1,0:T(8,128)(2,1)S(1)} %get-tuple-element.17.table_ref, ...), custom_call_target="tpu_custom_call" | custom-call | tf_op jit(solution)/shard_map/transform_other/pallas_call | solution.py:312
  39.8 9.6 %all_to_all.10.got_ref = bf16[4,320,128]{2,1,0:T(8,128)(2,1)S(1)} all-to-all(bf16[4,320,128]{2,1,0:T(8,128)(2,1)S(1)} %transform_other.1), channel_id=1, replica_groups={{4,2,6,0},{5,3,7,1},{12,10,14,8},{13,11,15,9},{20,18,22,16},{21,19,23,1..., dimensions={0} | all-to-all | bytes 655360 | tf_op jit(solution)/shard_map/all_to_all | solution.py:320
  49.4 0.8 %add.5 = f32[2,64,2,160]{3,2,1,0:T(2,128)} custom-call(bf16[4,320,128]{2,1,0:T(8,128)(2,1)S(1)} %all_to_all.10.got_ref), custom_call_target="tpu_custom_call" | custom-call | tf_op jit(solution)/shard_map/add/pallas_call | solution.py:323
Async XLA Ops:
  2.9 31.0 %all-to-all-start = ((bf16[64,6,2,128]{3,2,1,0:T(2,128)(2,1)}), bf16[64,6,2,128]{3,2,1,0:T(2,128)(2,1)S(1)}, u32[]{:S(2)}, u32[]{:S(2)}) async-start(bf16[64,6,2,128]{3,2,1,0:T(2,128)(2,1)} %bitcast.5), calls=%async_computation | async-start | bytes 393216 | tf_op jit(solution)/shard_map/all_to_all | solution.py:297
  24.3 0.7 %copy-start.2 = (s32[1280]{0:T(1024)S(1)}, s32[1280]{0:T(1024)}, u32[]{:S(2)}) copy-start(s32[1280]{0:T(1024)} %param.10) | copy-start | bytes 15364
  25.1 0.7 %copy-start = (s32[128]{0:T(128)S(1)}, s32[128]{0:T(128)}, u32[]{:S(2)}) copy-start(s32[128]{0:T(128)} %len_ref.1) | copy-start | bytes 1540
  25.1 0.7 %copy-start.1 = (s32[2]{0:T(128)S(1)}, s32[2]{0:T(128)}, u32[]{:S(2)}) copy-start(s32[2]{0:T(128)} %lat_ref.1) | copy-start | bytes 28
  33.8 4.9 %collective-permute-start = (bf16[768,128]{1,0:T(8,128)(2,1)S(1)}, bf16[768,128]{1,0:T(8,128)(2,1)S(1)}, u32[]{:S(2)}, u32[]{:S(2)}) collective-permute-start(bf16[768,128]{1,0:T(8,128)(2,1)S(1)} %bitcast.3), channel_id=1, source_target_pairs={{0,1},{1,0},{2,3},{3,2},{4,5},{5,4},{6,7},{7,6},{8,9},{9,8},{10,11... | collective-permute-start | bytes 589832 | tf_op jit(solution)/shard_map/ppermute | solution.py:302
